TPU v7x, 32 devices: a whole 2x2x4 slice. The times are simulated.
32 devices in a mesh: dp: 16 (over z, x, core), tensor: 2 (over y).
Axes of the slice: x: 2, y: 2, z: 4, core: 2. Of those that a mesh axis runs over, the one named last changes fastest.
Arguments:
- tokens_in: bfloat16 [24576, 768], P(('dp', 'tensor')), may hold values from -6 to 6
- seq_lengths: int32 [16, 3], P('dp'), may hold values from 1 to 1024, 1536 in all within a row
- norm1_gain: float32 [768], replicated, may hold values from 0.5 to 1.5
- norm2_gain: float32 [768], replicated, may hold values from 0.5 to 1.5
- w_qkv: bfloat16 [3, 768, 768], P(None, None, 'tensor'), may hold values from -0.21875 to 0.21875
- w_out: bfloat16 [768, 768], P('tensor'), may hold values from -0.625 to 0.625
- w_in: bfloat16 [2, 768, 1152], P(None, None, 'tensor'), may hold values from -0.21875 to 0.21875
- w_down: bfloat16 [1152, 768], P('tensor'), may hold values from -0.1875 to 0.1875
- out_grad: bfloat16 [24576, 768], P(('dp', 'tensor')), may hold values from -6 to 6
Outputs:
- out_tokens: bfloat16 [24576, 768], P(('dp', 'tensor'))
- in_grad: bfloat16 [24576, 768], P(('dp', 'tensor'))
- grad_norm1: float32 [768], replicated
- grad_norm2: float32 [768], replicated
- grad_qkv: float32 [3, 768, 768], P(None, None, 'tensor')
- grad_out: float32 [768, 768], P('tensor')
- grad_in: float32 [2, 768, 1152], P(None, None, 'tensor')
- grad_down: float32 [1152, 768], P('tensor')
Inputs may be any that keep to these rules, and one draw needn't show every extreme that they name: Each row of seq_lengths gives the lengths of the 3 sequences of one group in order; they sum to 1536, and the longest of each row is exactly 1024.
All inputs are finite; a program needn't handle non-finite values.
Results may differ from a plain program's by a relative error of at most 0.02.
Values may be sent and summed in bfloat16 or wider, within the bound.
No kernel may reach another device: no remote copies, remote signals or barrier semaphores. Data moves between devices by JAX's collectives and lax.ppermute only.
A program may use at most 128 MiB of HBM per device.

v0:
```python
import jax
import jax.numpy as jnp
from jax import lax
from jax.sharding import PartitionSpec as P

HEAD_DIM = 64
HALF = 64
BLOCK = 512


def places(lengths, group_rows):
    indices = jnp.arange(group_rows, dtype=jnp.int32)
    ends = jnp.cumsum(lengths)
    passed_end = indices[:, None] >= ends[None, :]
    segment = jnp.sum(passed_end.astype(jnp.int32), axis=1)
    opening = jnp.sum(jnp.where(passed_end, lengths[None, :], 0), axis=1)
    return (segment, indices - opening)


def rotations(position):
    frequency = 10000.0 ** (-jnp.arange(0, HEAD_DIM, 2, dtype=jnp.float32) / HEAD_DIM)
    angle_all = position.astype(jnp.float32)[:, None] * frequency[None, :]
    angle_all = jnp.concatenate([angle_all, angle_all], axis=1)[:, None, :]
    return (jnp.cos(angle_all), jnp.sin(angle_all))


def turn_half(values):
    half_dim = values.shape[-1] // 2
    return jnp.concatenate([-values[..., half_dim:], values[..., :half_dim]], axis=-1)


def rotate(values, cosine, sine_part):
    return values * cosine + turn_half(values) * sine_part


def unrotate(grads_back, cosine, sine_part):
    return grads_back * cosine - turn_half(grads_back * sine_part)


def normalize(values):
    centred = values - jnp.mean(values, axis=-1, keepdims=True)
    factor = lax.rsqrt(jnp.mean(centred * centred, axis=-1, keepdims=True) + 1e-05)
    return (centred * factor, factor)


def norm_back(d_norm, gain_vec, normed, factor):
    scaled = d_norm * gain_vec
    return factor * (
        scaled
        - jnp.mean(scaled, axis=-1, keepdims=True)
        - normed * jnp.mean(scaled * normed, axis=-1, keepdims=True)
    )


def window_mask(query_seg, key_seg, offset, step_rows):
    q_seg = lax.dynamic_slice_in_dim(query_seg, offset, step_rows)
    k_seg = lax.dynamic_slice_in_dim(key_seg, offset, step_rows + 2 * HALF)
    query_idx = jnp.arange(step_rows, dtype=jnp.int32)
    key_idx = jnp.arange(step_rows + 2 * HALF, dtype=jnp.int32) - HALF
    return (q_seg[:, None] == k_seg[None, :]) & (
        jnp.abs(query_idx[:, None] - key_idx[None, :]) <= HALF
    )


def block_scores(queries, keys_pad, query_seg, key_seg, offset, step_rows):
    q_block = lax.dynamic_slice_in_dim(queries, offset, step_rows, 0)
    k_block = lax.dynamic_slice_in_dim(keys_pad, offset, step_rows + 2 * HALF, 0)
    scores = jnp.einsum(
        "qhd,khd->hqk", q_block, k_block, preferred_element_type=jnp.float32
    ) * HEAD_DIM ** (-0.5)
    return (q_block, k_block, scores, window_mask(query_seg, key_seg, offset, step_rows))


def attend(queries, keys_pad, values_pad, query_seg, key_seg, step_rows):
    query_rows = queries.shape[0]

    def one_block(offset):
        q_block, k_block, scores, allowed = block_scores(
            queries, keys_pad, query_seg, key_seg, offset, step_rows
        )
        v_block = lax.dynamic_slice_in_dim(values_pad, offset, step_rows + 2 * HALF, 0)
        scores = jnp.where(allowed[None], scores, -1e30)
        peak_score = jnp.max(scores, axis=-1, keepdims=True)
        raw_weights = jnp.exp(scores - peak_score)
        totals = jnp.sum(raw_weights, axis=-1, keepdims=True)
        probability = raw_weights / totals
        mixed_rows = jnp.einsum(
            "hqk,khd->qhd",
            probability.astype(jnp.bfloat16),
            v_block,
            preferred_element_type=jnp.float32,
        )
        return (mixed_rows, (peak_score + jnp.log(totals))[..., 0])

    offsets = jnp.arange(query_rows // step_rows, dtype=jnp.int32) * step_rows
    mixed_rows, lse_all = lax.map(one_block, offsets)
    return (mixed_rows.reshape(query_rows, -1), lse_all)


def attend_back(queries, keys_pad, values_pad, query_seg, key_seg, lse_all, d_mixed, step_rows):
    query_rows = queries.shape[0]
    window_rows = step_rows + 2 * HALF
    score_scale = HEAD_DIM ** (-0.5)

    def one_block(pending, block_item):
        d_keys_pad, d_values_pad = pending
        offset, lse_block = block_item
        q_block, k_block, scores, allowed = block_scores(
            queries, keys_pad, query_seg, key_seg, offset, step_rows
        )
        v_block = lax.dynamic_slice_in_dim(values_pad, offset, window_rows, 0)
        probability = jnp.where(allowed[None], jnp.exp(scores - lse_block[..., None]), 0.0)
        prob_low = probability.astype(jnp.bfloat16)
        d_block = lax.dynamic_slice_in_dim(d_mixed, offset, step_rows, 0)
        d_probs = jnp.einsum("qhd,khd->hqk", d_block, v_block, preferred_element_type=jnp.float32)
        row_dot = jnp.sum(probability * d_probs, axis=-1, keepdims=True)
        d_scores = (probability * (d_probs - row_dot)).astype(jnp.bfloat16)
        d_query = score_scale * jnp.einsum(
            "hqk,khd->qhd", d_scores, k_block, preferred_element_type=jnp.float32
        )
        d_key = score_scale * jnp.einsum(
            "hqk,qhd->khd", d_scores, q_block, preferred_element_type=jnp.float32
        )
        d_value = jnp.einsum("hqk,qhd->khd", prob_low, d_block, preferred_element_type=jnp.float32)
        d_keys_pad = lax.dynamic_update_slice_in_dim(
            d_keys_pad,
            lax.dynamic_slice_in_dim(d_keys_pad, offset, window_rows, 0) + d_key,
            offset,
            0,
        )
        d_values_pad = lax.dynamic_update_slice_in_dim(
            d_values_pad,
            lax.dynamic_slice_in_dim(d_values_pad, offset, window_rows, 0) + d_value,
            offset,
            0,
        )
        return ((d_keys_pad, d_values_pad), d_query)

    empty_pad = jnp.zeros(keys_pad.shape, jnp.float32)
    offsets = jnp.arange(query_rows // step_rows, dtype=jnp.int32) * step_rows
    (d_keys_pad, d_values_pad), d_query = lax.scan(
        one_block, (empty_pad, empty_pad), (offsets, lse_all)
    )
    return (d_query.reshape(queries.shape), d_keys_pad, d_values_pad)


def row_product(left_rows, weights):
    return jnp.dot(left_rows, weights, preferred_element_type=jnp.float32)


def back_product(grads_stack, weights):
    return jnp.einsum("ktf,kdf->td", grads_stack, weights, preferred_element_type=jnp.float32)


def gelu_parts(up_in):
    cdf_part = 0.5 * (1.0 + jax.scipy.special.erf(up_in * 0.7071067811865476))
    gelu_out = up_in * cdf_part
    gelu_slope = cdf_part + up_in * jnp.exp(-0.5 * up_in * up_in) * 0.3989422804014327
    return (gelu_out, gelu_slope)


def per_device(
    tokens_in, seq_lengths, norm1_gain, norm2_gain, w_qkv, w_out, w_in, w_down, out_grad
):
    own_rows = tokens_in.shape[0]
    group_rows = own_rows * lax.axis_size("tensor")
    segment, position = places(seq_lengths[0], group_rows)
    tokens = tokens_in.astype(jnp.float32)
    normed_one, factor_one = normalize(tokens)
    norm1_low = (normed_one * norm1_gain).astype(jnp.bfloat16)
    cosine, sine_part = rotations(position)
    local_heads = w_qkv.shape[2] // HEAD_DIM
    head_shape = (group_rows, local_heads, HEAD_DIM)
    norm1_all = lax.all_gather(norm1_low, "tensor", axis=0, tiled=True)
    projected_qkv = jnp.einsum("td,kde->kte", norm1_all, w_qkv, preferred_element_type=jnp.float32)
    queries = rotate(projected_qkv[0].reshape(head_shape), cosine, sine_part).astype(jnp.bfloat16)
    keys_all = rotate(projected_qkv[1].reshape(head_shape), cosine, sine_part).astype(jnp.bfloat16)
    values_all = projected_qkv[2].reshape(head_shape).astype(jnp.bfloat16)
    keys_pad = jnp.pad(keys_all, ((HALF, HALF), (0, 0), (0, 0)))
    values_pad = jnp.pad(values_all, ((HALF, HALF), (0, 0), (0, 0)))
    key_seg = jnp.pad(segment, (HALF, HALF), constant_values=-1)
    mixed_full, lse_all = attend(queries, keys_pad, values_pad, segment, key_seg, BLOCK)
    mixed_low = mixed_full.astype(jnp.bfloat16)
    attn_share = lax.psum_scatter(
        row_product(mixed_low, w_out).astype(jnp.bfloat16),
        "tensor",
        scatter_dimension=0,
        tiled=True,
    ).astype(jnp.float32)
    residual = tokens + attn_share
    normed_two, factor_two = normalize(residual)
    norm2_low = (normed_two * norm2_gain).astype(jnp.bfloat16)
    norm2_all = lax.all_gather(norm2_low, "tensor", axis=0, tiled=True)
    projected_in = jnp.einsum("td,kdf->ktf", norm2_all, w_in, preferred_element_type=jnp.float32)
    up_in = projected_in[0]
    gate_vals = projected_in[1]
    gelu_out, gelu_slope = gelu_parts(up_in)
    act_low = (gelu_out * gate_vals).astype(jnp.bfloat16)
    mlp_share = lax.psum_scatter(
        row_product(act_low, w_down).astype(jnp.bfloat16), "tensor", scatter_dimension=0, tiled=True
    ).astype(jnp.float32)
    out_tokens = (residual + mlp_share).astype(jnp.bfloat16)
    d_out_all = lax.all_gather(out_grad, "tensor", axis=0, tiled=True)
    grad_down = jnp.einsum("tf,td->fd", act_low, d_out_all, preferred_element_type=jnp.float32)
    d_act = jnp.einsum("td,fd->tf", d_out_all, w_down, preferred_element_type=jnp.float32)
    d_up = jnp.stack([d_act * gate_vals * gelu_slope, d_act * gelu_out]).astype(jnp.bfloat16)
    grad_in = jnp.einsum("td,ktf->kdf", norm2_all, d_up, preferred_element_type=jnp.float32)
    d_norm2 = lax.psum_scatter(
        back_product(d_up, w_in).astype(jnp.bfloat16), "tensor", scatter_dimension=0, tiled=True
    ).astype(jnp.float32)
    grad_norm2 = jnp.sum(d_norm2 * normed_two, axis=0)
    d_res = out_grad.astype(jnp.float32) + norm_back(d_norm2, norm2_gain, normed_two, factor_two)
    d_attn_all = lax.all_gather(d_res.astype(jnp.bfloat16), "tensor", axis=0, tiled=True)
    grad_out = jnp.einsum("te,td->ed", mixed_low, d_attn_all, preferred_element_type=jnp.float32)
    d_mixed = jnp.einsum("td,ed->te", d_attn_all, w_out, preferred_element_type=jnp.float32)
    d_mixed = d_mixed.astype(jnp.bfloat16).reshape(head_shape)
    d_query, d_keys_pad, d_values_pad = attend_back(
        queries, keys_pad, values_pad, segment, key_seg, lse_all, d_mixed, BLOCK
    )
    d_key = d_keys_pad[HALF : HALF + group_rows]
    d_value = d_values_pad[HALF : HALF + group_rows]
    d_raw = jnp.stack(
        [
            unrotate(d_query, cosine, sine_part).reshape(group_rows, -1),
            unrotate(d_key, cosine, sine_part).reshape(group_rows, -1),
            d_value.reshape(group_rows, -1),
        ]
    ).astype(jnp.bfloat16)
    grad_qkv = jnp.einsum("td,kte->kde", norm1_all, d_raw, preferred_element_type=jnp.float32)
    d_norm1 = lax.psum_scatter(
        back_product(d_raw, w_qkv).astype(jnp.bfloat16), "tensor", scatter_dimension=0, tiled=True
    ).astype(jnp.float32)
    grad_norm1 = jnp.sum(d_norm1 * normed_one, axis=0)
    in_grad = (d_res + norm_back(d_norm1, norm1_gain, normed_one, factor_one)).astype(jnp.bfloat16)
    grad_qkv, grad_out, grad_in, grad_down = lax.psum(
        (grad_qkv, grad_out, grad_in, grad_down), "dp"
    )
    grad_norm1, grad_norm2 = lax.psum((grad_norm1, grad_norm2), ("dp", "tensor"))
    return (out_tokens, in_grad, grad_norm1, grad_norm2, grad_qkv, grad_out, grad_in, grad_down)


def solution(mesh):
    in_specs = (
        P(("dp", "tensor"), None),
        P("dp", None),
        P(),
        P(),
        P(None, None, "tensor"),
        P("tensor", None),
        P(None, None, "tensor"),
        P("tensor", None),
        P(("dp", "tensor"), None),
    )
    out_specs = (
        P(("dp", "tensor"), None),
        P(("dp", "tensor"), None),
        P(),
        P(),
        P(None, None, "tensor"),
        P("tensor", None),
        P(None, None, "tensor"),
        P("tensor", None),
    )
    return jax.shard_map(
        per_device, mesh=mesh, in_specs=in_specs, out_specs=out_specs, check_vma=False
    )
```

profile of v0, /device:TPU:1, one launch (start us, length us, event | category | flops | bytes accessed | tf_op | source)
XLA Modules:
  0.0 763.7 jit_solution(16553373418642408953)
XLA Ops:
  16.5 34.5 %all-gather.5.cloned.1.call-done = bf16[1536,768]{1,0:T(8,128)(2,1)} async-done(((bf16[768,768]{1,0:T(8,128)(2,1)}), bf16[1536,768]{1,0:T(8,128)(2,1)}) %all-gather.5.cloned.1.call-update) | async-done | bytes 2359312 | tf_op jit(solution)/shard_map/all_gather | solution.py:174
  51.1 5.4 convolution_bitcast_fusion.1
  63.4 44.1 %while.32 = (s32[]{:T(128)}, bf16[3,512,6,64]{1,3,2,0:T(8,128)(2,1)}, f32[3,6,512]{2,1,0:T(8,128)S(1)}, s32[3]{0:T(128)S(1)}, bf16[1664,6,64]{0,2,1:T(8,128)(2,1...) while((s32[]{:T(128)}, ...), condition=%wide.region_8.9_spmd.clone, body=%wide.region_5.8_spmd.sunk.clone | while | flops 528545408 | bytes 36641536 | solution.py:96
  114.2 34.8 %reduce-scatter.5.cloned.1.call-done = bf16[768,768]{1,0:T(8,128)(2,1)} async-done(((bf16[1536,768]{1,0:T(8,128)(2,1)}), bf16[768,768]{1,0:T(8,128)(2,1)}) %reduce-scatter.5.cloned.1.call-update) | async-done | bytes 1179664 | tf_op jit(solution)/shard_map/reduce_scatter | solution.py:184
  153.6 35.6 %all-gather.7.cloned.1.call-done = bf16[1536,768]{1,0:T(8,128)(2,1)} async-done(((bf16[768,768]{1,0:T(8,128)(2,1)}), bf16[1536,768]{1,0:T(8,128)(2,1)}) %all-gather.7.cloned.1.call-update) | async-done | bytes 2359312 | tf_op jit(solution)/shard_map/all_gather | solution.py:193
  189.2 6.6 convolution_bitcast_fusion
  195.8 31.0 %all-gather.9.cloned.1.call-done = bf16[1536,768]{1,0:T(8,128)(2,1)} async-done(((bf16[768,768]{1,0:T(8,128)(2,1)}), bf16[1536,768]{1,0:T(8,128)(2,1)}) %all-gather.9.cloned.1.call-update) | async-done | bytes 2359312 | tf_op jit(solution)/shard_map/all_gather | solution.py:203
  226.8 6.9 fusion.94
  240.1 34.8 %reduce-scatter.9.cloned.1.call-done = bf16[768,768]{1,0:T(8,128)(2,1)} async-done(((bf16[1536,768]{1,0:T(8,128)(2,1)}), bf16[768,768]{1,0:T(8,128)(2,1)}) %reduce-scatter.9.cloned.1.call-update) | async-done | bytes 1179664 | tf_op jit(solution)/shard_map/reduce_scatter | solution.py:208
  286.5 31.3 %all-gather.11.cloned.1.call-done = bf16[1536,768]{1,0:T(8,128)(2,1)} async-done(((bf16[768,768]{1,0:T(8,128)(2,1)}), bf16[1536,768]{1,0:T(8,128)(2,1)}) %all-gather.11.cloned.1.call-update) | async-done | bytes 2359312 | tf_op jit(solution)/shard_map/all_gather | solution.py:213
  324.8 110.3 %while.33 = (s32[]{:T(128)}, f32[1664,6,64]{0,2,1:T(8,128)}, f32[1664,6,64]{0,2,1:T(8,128)}, f32[3,512,6,64]{1,3,2,0:T(8,128)}, s32[3]{0:T(128)S(1)}, /*index=5*...) while((s32[]{:T(128)}, f32[1664,6,64]{0,2,1:T(8,128)}, ...), condition=%wide.region_18.19_spmd.clone, body=%wide.region_16.18_spmd.sunk.clone | while | flops 1290352256 | bytes 135011152 | solution.py:141
  343.0 7.2 multiply_reduce_fusion.4
  380.3 7.2 multiply_reduce_fusion.4
  416.7 7.1 multiply_reduce_fusion.4
  438.8 5.4 copy.49
  458.3 5.7 reshape.339
  473.3 5.2 convolution_convert_fusion
  478.9 5.8 fusion.104
  491.5 4.9 fusion.86
  496.5 11.6 %reduce-scatter.11.cloned.1.call-done = bf16[768,768]{1,0:T(8,128)(2,1)} async-done(((bf16[1536,768]{1,0:T(8,128)(2,1)}), bf16[768,768]{1,0:T(8,128)(2,1)}) %reduce-scatter.11.cloned.1.call-update) | async-done | bytes 1179664 | tf_op jit(solution)/shard_map/reduce_scatter | solution.py:230
  510.6 39.2 %all-reduce.3 = (f32[768]{0:T(1024)}, f32[768]{0:T(1024)}) all-reduce(f32[768]{0:T(1024)S(1)} %get-tuple-element.304, f32[768]{0:T(1024)S(1)} %copy-done.41), channel_id=1, replica_groups=mesh['dp'=16,'tensor'=2] {'dp','tensor'}, use_global_device_ids=true, to_apply=%region_23.24 | all-reduce | flops 1536 | bytes 12288 | tf_op jit(solution)/shard_map/psum | solution.py:238
  549.9 4.8 fusion.66
  554.7 190.3 %all-reduce.7.cloned.1.call-done = (f32[3,768,384]{1,2,0:T(8,128)}, f32[384,768]{1,0:T(8,128)}, f32[2,768,576]{1,2,0:T(8,128)}, f32[576,768]{1,0:T(8,128)}) async-done(((f32[3,768,384]{1,2,0:T(8,128)}, f32[384,768]{1,0:T(8,128)}, f32[2,768,576]{1,2,0:T(8,128)}, f32[576,768]{1,0:T(8,128)}), (f32[3,768,384]{1,2,0:T(8,128)}, f32[384,768]{1,0:T(8,128)}, f32[2,768,576]{1,2,0:T(8,128)}, ...) | async-done | bytes 10027024 | tf_op jit(solution)/shard_map/psum | solution.py:235
  745.1 5.2 copy.46
  (267 shorter events, 208.5 us)
Async XLA Ops:
  7.2 182.0 %copy-start = (bf16[2,768,576]{1,2,0:T(8,128)(2,1)S(1)}, bf16[2,768,576]{1,2,0:T(8,128)(2,1)}, u32[]{:S(2)}) copy-start(bf16[2,768,576]{1,2,0:T(8,128)(2,1)} %param.19) | copy-start | bytes 5308420
  7.2 43.9 %all-gather.5.cloned.1.call-start = ((), (), s32[]{:S(2)}) async-start(), calls=%async_computation.4 | async-start | bytes 3538944 | tf_op jit(solution)/shard_map/all_gather | solution.py:174
  12.8 136.2 %reduce-scatter.5.cloned.1.call-start = ((), (), s32[]{:S(2)}) async-start(), calls=%async_computation.5 | async-start | bytes 3538944 | tf_op jit(solution)/shard_map/reduce_scatter | solution.py:184
  114.1 37.3 %copy-start.33 = (f32[768]{0:T(1024)S(1)}, f32[768]{0:T(1024)}, u32[]{:S(2)}) copy-start(f32[768]{0:T(1024)} %param.16) | copy-start | bytes 9220
  114.1 75.1 %all-gather.7.cloned.1.call-start = ((), (), s32[]{:S(2)}) async-start(), calls=%async_computation.6 | async-start | bytes 3538944 | tf_op jit(solution)/shard_map/all_gather | solution.py:193
  150.7 127.5 %copy-start.25 = (f32[768]{0:T(1024)}, f32[768]{0:T(1024)S(1)}, u32[]{:S(2)}) copy-start(f32[768]{0:T(1024)S(1)} %broadcast_multiply_fusion.6) | copy-start | bytes 9220
  151.4 126.8 %copy-start.29 = (f32[768]{0:T(1024)}, f32[768]{0:T(1024)S(1)}, u32[]{:S(2)}) copy-start(f32[768]{0:T(1024)S(1)} %add_rsqrt_fusion) | copy-start | bytes 9220
  153.0 73.8 %all-gather.9.cloned.1.call-start = ((), (), s32[]{:S(2)}) async-start(), calls=%async_computation.8 | async-start | bytes 3538944 | tf_op jit(solution)/shard_map/all_gather | solution.py:203
  153.5 121.4 %reduce-scatter.9.cloned.1.call-start = ((), (), s32[]{:S(2)}) async-start(), calls=%async_computation.9 | async-start | bytes 3538944 | tf_op jit(solution)/shard_map/reduce_scatter | solution.py:208
  240.1 34.9 %copy-start.10 = (bf16[768,768]{1,0:T(8,128)(2,1)S(1)}, bf16[768,768]{1,0:T(8,128)(2,1)}, u32[]{:S(2)}) copy-start(bf16[768,768]{1,0:T(8,128)(2,1)} %reduce-scatter.5.cloned.1.call-done) | copy-start | bytes 3538948
  240.1 77.6 %all-gather.11.cloned.1.call-start = ((), (), s32[]{:S(2)}) async-start(), calls=%async_computation.10 | async-start | bytes 3538944 | tf_op jit(solution)/shard_map/all_gather | solution.py:213
  281.5 226.6 %reduce-scatter.11.cloned.1.call-start = ((), (), s32[]{:S(2)}) async-start(), calls=%async_computation.11 | async-start | bytes 3538944 | tf_op jit(solution)/shard_map/reduce_scatter | solution.py:230
  283.2 34.5 %copy-start.48 = (bf16[384,768]{1,0:T(8,128)(2,1)S(1)}, bf16[384,768]{1,0:T(8,128)(2,1)}, u32[]{:S(2)}) copy-start(bf16[384,768]{1,0:T(8,128)(2,1)} %param.18) | copy-start | bytes 1769476
  473.3 76.6 %reduce-scatter.7.cloned.1.call-start = ((), (), s32[]{:S(2)}) async-start(), calls=%async_computation.7 | async-start | bytes 3538944 | tf_op jit(solution)/shard_map/reduce_scatter | solution.py:199
  478.5 266.5 %all-reduce.7.cloned.1.call-start = ((), (), s32[]{:S(2)}) async-start(), calls=%async_computation.12 | async-start | bytes 20054016 | tf_op jit(solution)/shard_map/psum | solution.py:235
  496.4 11.7 %copy-start.32 = (f32[768]{0:T(1024)S(1)}, f32[768]{0:T(1024)}, u32[]{:S(2)}) copy-start(f32[768]{0:T(1024)} %copy-done.31) | copy-start | bytes 9220
  496.4 11.7 %copy-start.36 = (f32[768]{0:T(1024)S(1)}, f32[768]{0:T(1024)}, u32[]{:S(2)}) copy-start(f32[768]{0:T(1024)} %param.15) | copy-start | bytes 9220
  496.5 14.2 %copy-start.41 = (f32[768]{0:T(1024)S(1)}, f32[768]{0:T(1024)}, u32[]{:S(2)}) copy-start(f32[768]{0:T(1024)} %get-tuple-element.302) | copy-start | bytes 9220
  496.5 53.4 %copy-start.11 = (bf16[768,768]{1,0:T(8,128)(2,1)S(1)}, bf16[768,768]{1,0:T(8,128)(2,1)}, u32[]{:S(2)}) copy-start(bf16[768,768]{1,0:T(8,128)(2,1)} %reduce-scatter.5.cloned.1.call-done) | copy-start | bytes 3538948
  496.5 53.4 %copy-start.26 = (f32[768]{0:T(1024)S(1)}, f32[768]{0:T(1024)}, u32[]{:S(2)}) copy-start(f32[768]{0:T(1024)} %copy-done.25) | copy-start | bytes 9220
  496.5 53.4 %copy-start.30 = (f32[768]{0:T(1024)S(1)}, f32[768]{0:T(1024)}, u32[]{:S(2)}) copy-start(f32[768]{0:T(1024)} %copy-done.29) | copy-start | bytes 9220
  496.5 53.4 %copy-start.34 = (f32[768]{0:T(1024)S(1)}, f32[768]{0:T(1024)}, u32[]{:S(2)}) copy-start(f32[768]{0:T(1024)} %param.16) | copy-start | bytes 9220
  496.5 53.4 %copy-start.38 = (f32[768]{0:T(1024)S(1)}, f32[768]{0:T(1024)}, u32[]{:S(2)}) copy-start(f32[768]{0:T(1024)} %copy-done.37) | copy-start | bytes 9220
  496.5 53.4 %copy-start.40 = (f32[768]{0:T(1024)S(1)}, f32[768]{0:T(1024)}, u32[]{:S(2)}) copy-start(f32[768]{0:T(1024)} %copy-done.39) | copy-start | bytes 9220
  (46 other events, 170.1 us)
Sparse Core Ops, SparseCore 0:
  12.9 38.1 all-gather.4
  114.2 34.7 reduce-scatter.4
  153.1 36.0 all-gather.6
  190.7 36.0 all-gather.8
  240.2 34.6 reduce-scatter.8
  281.6 36.0 all-gather.10
  473.4 34.7 reduce-scatter.10
  510.5 35.3 reduce-scatter.6
  550.5 194.4 all-reduce.6
where the time goes:
time: 776 us; the launch traced here: 764 us
  waiting for transfers between devices  405 us (52%)
  matrix products  131 us (17%)
  local copies, waits for them, and re-layouts  97.8 us (13%)
  other arithmetic  55.7 us (7%)
  blocking collectives  39.2 us (5%)
  loops' own time  19.8 us (3%)
  between operations  14.8 us (2%)
    psum x1, waiting for transfers between devices, per_device(): lax.psum((grad_qkv, grad_out, grad_in, grad_down), 'dp')  190 us
    psum x1, blocking collectives, per_device(): lax.psum((grad_norm1, grad_norm2), ('dp', 'tensor'))  39.2 us
    all_gather x1, waiting for transfers between devices, per_device(): norm2_all = lax.all_gather(norm2_low, 'tensor', axis=0, tiled=True)  35.6 us
    reduce_scatter x1, waiting for transfers between devices, per_device(): lax.psum_scatter(back_product(d_up, w_in).astype(jnp.bfloat16), 'tensor',...  34.8 us
    reduce_scatter x1, waiting for transfers between devices, per_device(): lax.psum_scatter(row_product(mixed_low, w_out).astype(jnp.bfloat16), 'ten...  34.8 us
    all_gather x1, waiting for transfers between devices, per_device(): norm1_all = lax.all_gather(norm1_low, 'tensor', axis=0, tiled=True)  34.5 us
    all_gather x1, waiting for transfers between devices, per_device(): lax.all_gather(d_res.astype(jnp.bfloat16), 'tensor', axis=0, tiled=True)  31.3 us
    all_gather x1, waiting for transfers between devices, per_device(): d_out_all = lax.all_gather(out_grad, 'tensor', axis=0, tiled=True)  31 us
  transfers between devices with their start and end apart: 9, of which 8 were waited for; matrix products, arithmetic and copies ran while one was open for 6% of the time, Pallas kernels for 0%

commit v1 on v0

v1 whole, which is shorter than its diff:
```python
import functools

import jax
import jax.numpy as jnp
from jax import lax
from jax.experimental import pallas as pl
from jax.experimental.pallas import tpu as pltpu
from jax.sharding import Mesh, PartitionSpec as P

HEAD_DIM = 64
HALF = 64
QB = 128
WIN = QB + 2 * HALF
SWAP = [(0, 1), (1, 0)]
BF = jnp.bfloat16
F32 = jnp.float32


def vmem(megabytes):
    return pltpu.CompilerParams(vmem_limit_bytes=megabytes * 1024 * 1024)


def spread_tables(rows, index, lengths):
    ends = jnp.cumsum(lengths)
    passed = index[:, None] >= ends[None, :]
    opening = jnp.sum(jnp.where(passed, lengths[None, :], 0), axis=1)
    position = (index - opening).astype(F32)
    frequency = 10000.0 ** (-jnp.arange(0, HEAD_DIM, 2, dtype=F32) / HEAD_DIM)
    angle = position[:, None] * frequency[None, :]
    cosine, sine = jnp.cos(angle), jnp.sin(angle)
    return (
        jnp.concatenate([cosine] * 4, axis=1),
        jnp.concatenate([-sine, sine, -sine, sine], axis=1),
    )


def normalize(values):
    centred = values - jnp.mean(values, axis=-1, keepdims=True)
    factor = lax.rsqrt(jnp.mean(centred * centred, axis=-1, keepdims=True) + 1e-05)
    return (centred * factor, factor)


def norm_back(d_norm, gain_vec, normed, factor):
    scaled = d_norm * gain_vec
    return factor * (
        scaled
        - jnp.mean(scaled, axis=-1, keepdims=True)
        - normed * jnp.mean(scaled * normed, axis=-1, keepdims=True)
    )


def partner_lanes(values):
    lane = lax.broadcasted_iota(jnp.int32, values.shape, 1)
    lower = (lane & 32) == 0
    width = values.shape[1]
    return jnp.where(
        lower, pltpu.roll(values, width - 32, 1), pltpu.roll(values, 32, 1)
    )


def window_bias(scal_ref, block, rows):
    e0, e1, t0, h0 = scal_ref[0], scal_ref[1], scal_ref[2], scal_ref[3]
    j = block * QB + lax.broadcasted_iota(jnp.int32, (WIN, QB), 0)
    t = t0 + block * QB + lax.broadcasted_iota(jnp.int32, (WIN, QB), 1)
    u = jnp.where(
        j < HALF, h0 + j, jnp.where(j >= rows + HALF, h0 + j - rows - HALF, t0 + j - HALF)
    )
    seg_t = (t >= e0).astype(jnp.int32) + (t >= e1).astype(jnp.int32)
    seg_u = (u >= e0).astype(jnp.int32) + (u >= e1).astype(jnp.int32)
    allowed = (seg_t == seg_u) & (jnp.abs(t - u) <= HALF)
    bias = jnp.where(allowed, 0.0, -1e30).astype(F32)
    return jnp.concatenate([bias, bias], axis=1)


def stack_heads(pair):
    lower = lax.broadcasted_iota(jnp.int32, pair.shape, 1) < HEAD_DIM
    zero = jnp.zeros_like(pair)
    return jnp.concatenate(
        [jnp.where(lower, pair, zero), jnp.where(lower, zero, pair)], axis=0
    )


def unstack_columns(both):
    return jnp.concatenate(
        [both[:HEAD_DIM, :QB], both[HEAD_DIM:, QB:]], axis=0
    ).T


def dot(a, b, contract):
    return lax.dot_general(a, b, ((contract[0], contract[1]), ((), ())), preferred_element_type=F32)


def qkv_attn_kernel(
    scal_ref, norm_ref, w_ref, cos_ref, sin_ref, q_ref, k_ref, v_ref, mixed_ref, lse_ref
):
    rows = q_ref.shape[0]
    ext = norm_ref.shape[0]
    width = q_ref.shape[1]
    pairs = width // 128
    step = 208 if ext % 208 == 0 else 64

    def project(i, carry):
        at = pl.ds(pl.multiple_of(i * step, 16), step)
        low = norm_ref[at, :]
        cos, sin = cos_ref[at, :], sin_ref[at, :]
        raw_q = jnp.dot(low, w_ref[0], preferred_element_type=F32)
        raw_k = jnp.dot(low, w_ref[1], preferred_element_type=F32)
        raw_v = jnp.dot(low, w_ref[2], preferred_element_type=F32)
        out = pl.ds(pl.multiple_of(HALF + i * step, 16), step)
        for p in range(pairs):
            cols = slice(p * 128, (p + 1) * 128)
            part = raw_q[:, cols]
            qp = (part * cos + partner_lanes(part) * sin).astype(BF) * BF(HEAD_DIM**-0.5)
            qs_ref = q_all
            qs_ref[at, cols] = qp
            part = raw_k[:, cols]
            k_ref[out, cols] = (part * cos + partner_lanes(part) * sin).astype(BF)
        v_ref[out, :] = raw_v.astype(BF)
        return carry

    def run(q_scr):
        nonlocal q_all
        q_all = q_scr
        lax.fori_loop(0, ext // step, project, 0)
        q_ref[...] = q_scr[:rows, :]

    q_all = None
    pl.run_scoped(run, pltpu.VMEM((ext, width), BF))
    k_ref[:HALF, :] = k_ref[rows + HALF :, :]
    v_ref[:HALF, :] = v_ref[rows + HALF :, :]

    def block(i, carry):
        bias = window_bias(scal_ref, i, rows)
        at = pl.ds(pl.multiple_of(i * QB, QB), QB)
        keys = pl.ds(pl.multiple_of(i * QB, QB), WIN)
        for p in range(pairs):
            cols = slice(p * 128, (p + 1) * 128)
            qs = stack_heads(q_ref[at, cols])
            scores = dot(k_ref[keys, cols], qs, ((1,), (1,))) + bias
            peak = jnp.max(scores, axis=0, keepdims=True)
            raw = jnp.exp(scores - peak)
            total = jnp.sum(raw, axis=0, keepdims=True)
            probs = (raw * (1.0 / total)).astype(BF)
            both = dot(v_ref[keys, cols], probs, ((0,), (0,)))
            mixed_ref[at, cols] = unstack_columns(both).astype(BF)
            lse_ref[i, p] = peak + jnp.log(total)
        return carry

    lax.fori_loop(0, rows // QB, block, 0)


def qkv_attn(scal, norm_ext, w, cos, sin, rows):
    ext = norm_ext.shape[0]
    width = w.shape[2]
    whole = pl.BlockSpec(memory_space=pltpu.VMEM)
    return pl.pallas_call(
        qkv_attn_kernel,
        out_shape=(
            jax.ShapeDtypeStruct((rows, width), BF),
            jax.ShapeDtypeStruct((rows + 2 * HALF, width), BF),
            jax.ShapeDtypeStruct((rows + 2 * HALF, width), BF),
            jax.ShapeDtypeStruct((rows, width), BF),
            jax.ShapeDtypeStruct((rows // QB, width // 128, 1, 2 * QB), F32),
        ),
        in_specs=[pl.BlockSpec(memory_space=pltpu.SMEM)] + [whole] * 4,
        out_specs=(whole,) * 5,
        compiler_params=vmem(28),
        cost_estimate=pl.CostEstimate(
            flops=2 * ext * norm_ext.shape[1] * 3 * width + 16 * rows * WIN * width,
            bytes_accessed=8_000_000,
            transcendentals=rows * WIN * width // 64,
        ),
        name="qkv_attn",
    )(scal, norm_ext, w, cos, sin)


def attn_back_kernel(
    scal_ref, q_ref, k_ref, v_ref, dm_ref, lse_ref, cos_ref, sin_ref,
    dq_ref, dk_ref, dv_ref, dk_acc, dv_acc,
):
    rows = q_ref.shape[0]
    pairs = q_ref.shape[1] // 128
    dk_acc[...] = jnp.zeros_like(dk_acc)
    dv_acc[...] = jnp.zeros_like(dv_acc)

    def unrotate(part, at):
        return (part * cos_ref[at, :] - partner_lanes(part) * sin_ref[at, :]).astype(BF)

    def block(i, carry):
        bias = window_bias(scal_ref, i, rows)
        at = pl.ds(pl.multiple_of(i * QB, QB), QB)
        keys = pl.ds(pl.multiple_of(i * QB, QB), WIN)
        for p in range(pairs):
            cols = slice(p * 128, (p + 1) * 128)
            qs = stack_heads(q_ref[at, cols])
            ds_mixed = stack_heads(dm_ref[at, cols])
            kb = k_ref[keys, cols]
            vb = v_ref[keys, cols]
            scores = dot(kb, qs, ((1,), (1,))) + bias
            probs = jnp.exp(scores - lse_ref[i, p])
            d_probs = dot(vb, ds_mixed, ((1,), (1,)))
            row_dot = jnp.sum(probs * d_probs, axis=0, keepdims=True)
            d_scores = (probs * (d_probs - row_dot)).astype(BF)
            dk_acc[keys, cols] += dot(d_scores, qs, ((1,), (0,)))
            dv_acc[keys, cols] += dot(probs.astype(BF), ds_mixed, ((1,), (0,)))
            both = dot(kb, d_scores, ((0,), (0,)))
            dq = unstack_columns(both) * HEAD_DIM**-0.5
            dq_ref[at, cols] = unrotate(dq, at)
        return carry

    lax.fori_loop(0, rows // QB, block, 0)
    dk_acc[rows + HALF :, :] += dk_acc[:HALF, :]
    dv_acc[rows + HALF :, :] += dv_acc[:HALF, :]

    def finish(i, carry):
        at = pl.ds(pl.multiple_of(i * HALF, HALF), HALF)
        src = pl.ds(pl.multiple_of(HALF + i * HALF, HALF), HALF)
        for p in range(pairs):
            cols = slice(p * 128, (p + 1) * 128)
            dk_ref[at, cols] = unrotate(dk_acc[src, cols], at)
        dv_ref[at, :] = dv_acc[src, :].astype(BF)
        return carry

    lax.fori_loop(0, rows // HALF + 1, finish, 0)


def attn_back(scal, q, k, v, dm, lse, cos, sin):
    rows, width = q.shape
    whole = pl.BlockSpec(memory_space=pltpu.VMEM)
    return pl.pallas_call(
        attn_back_kernel,
        out_shape=(
            jax.ShapeDtypeStruct((rows, width), BF),
            jax.ShapeDtypeStruct((rows + HALF, width), BF),
            jax.ShapeDtypeStruct((rows + HALF, width), BF),
        ),
        in_specs=[pl.BlockSpec(memory_space=pltpu.SMEM)] + [whole] * 7,
        out_specs=(whole,) * 3,
        scratch_shapes=[pltpu.VMEM((rows + 2 * HALF, width), F32)] * 2,
        compiler_params=vmem(28),
        cost_estimate=pl.CostEstimate(
            flops=40 * rows * WIN * width,
            bytes_accessed=8_000_000,
            transcendentals=rows * WIN * width // 64,
        ),
        name="attn_back",
    )(scal, q, k, v, dm, lse, cos, sin)


def gelu_parts(up_in):
    cdf_part = 0.5 * (1.0 + lax.erf(up_in * 0.7071067811865476))
    gelu_out = up_in * cdf_part
    gelu_slope = cdf_part + up_in * jnp.exp(-0.5 * up_in * up_in) * 0.3989422804014327
    return (gelu_out, gelu_slope)


def mm(a, b):
    return jnp.dot(a, b, preferred_element_type=F32)


def mm_nt(a, b):
    return lax.dot_general(a, b, (((1,), (1,)), ((), ())), preferred_element_type=F32)


def mm_tn(a, b):
    return lax.dot_general(a, b, (((0,), (0,)), ((), ())), preferred_element_type=F32)


def pick(core, array, dim):
    size = array.shape[dim] // 2
    return lax.dynamic_slice_in_dim(array, core * size, size, dim)


def join(core, mine, other, dim):
    return jnp.where(
        core == 0,
        jnp.concatenate([mine, other], axis=dim),
        jnp.concatenate([other, mine], axis=dim),
    )


def fetch(core, array, dim):
    across = lax.ppermute(pick(core, array, dim), "tensor", SWAP)
    beside = lax.ppermute(across, "core", SWAP)
    return join(core, across, beside, dim)


def over_cores(core, array):
    recv = lax.ppermute(pick(1 - core, array, 0), "core", SWAP)
    return pick(core, array, 0).astype(F32) + recv.astype(F32)


def over_chips(core, array):
    chips = lax.axis_size("chip")
    rows, width = array.shape
    pieces = array.astype(BF).reshape(chips, rows // chips, width)
    pieces = lax.all_to_all(pieces, "chip", 0, 0)
    total = jnp.sum(pieces.astype(F32), axis=0).astype(BF)
    spread = jnp.broadcast_to(total[None], (chips,) + total.shape)
    full = lax.all_to_all(spread, "chip", 0, 0).reshape(rows, width)
    beside = lax.ppermute(full, "core", SWAP)
    return join(core, full, beside, 0)


def per_device(
    tokens_in, seq_lengths, norm1_gain, norm2_gain, w_qkv, w_out, w_in, w_down, out_grad
):
    rows, width = tokens_in.shape
    tensor = lax.axis_index("tensor")
    core = lax.axis_index("core")
    ff = w_in.shape[2]

    edge = jnp.where(tensor == 0, tokens_in[rows - HALF :], tokens_in[:HALF])
    halo = lax.ppermute(edge, "tensor", SWAP)
    w_qkv_x = fetch(core, w_qkv, 1)
    w_out_x = fetch(core, w_out, 0)
    w_in_x = fetch(core, w_in, 1)
    w_down_x = fetch(core, w_down, 0)

    lengths = seq_lengths[0]
    own0 = tensor * rows
    halo0 = jnp.where(tensor == 0, rows, rows - HALF)
    index = jnp.concatenate(
        [own0 + jnp.arange(rows, dtype=jnp.int32), halo0 + jnp.arange(HALF, dtype=jnp.int32)]
    )
    cos, sin = spread_tables(rows, index, lengths)
    scal = jnp.stack(
        [lengths[0], lengths[0] + lengths[1], own0, halo0]
    ).astype(jnp.int32)

    tokens_ext = jnp.concatenate([tokens_in, halo], axis=0).astype(F32)
    normed_one, factor_one = normalize(tokens_ext)
    norm1 = (normed_one * norm1_gain).astype(BF)

    q_o, k_o, v_o, mixed_o, lse_o = qkv_attn(scal, norm1, w_qkv, cos, sin, rows)
    q_x, k_x, v_x, mixed_x, lse_x = qkv_attn(scal, norm1, w_qkv_x, cos, sin, rows)

    tokens = tokens_in.astype(F32)
    residual = tokens + (mm(mixed_o, w_out) + mm(mixed_x, w_out_x))
    normed_two, factor_two = normalize(residual)
    norm2 = (normed_two * norm2_gain).astype(BF)

    def ffn(win, wdown):
        up_in = mm(norm2, win[0])
        gate = mm(norm2, win[1])
        gelu_out, gelu_slope = gelu_parts(up_in)
        act = (gelu_out * gate).astype(BF)
        share = mm(act, wdown)
        d_act = mm_nt(out_grad, wdown)
        d_up = (d_act * gate * gelu_slope).astype(BF)
        d_gate = (d_act * gelu_out).astype(BF)
        d_norm = mm_nt(d_up, win[0]) + mm_nt(d_gate, win[1])
        grads = jnp.concatenate(
            [
                mm_tn(norm2, d_up).astype(BF),
                mm_tn(norm2, d_gate).astype(BF),
                mm_tn(out_grad, act).astype(BF),
            ],
            axis=1,
        )
        return share, d_norm, grads

    share_o, d_norm2_o, ff_o = ffn(w_in, w_down)
    share_x, d_norm2_x, ff_x = ffn(w_in_x, w_down_x)
    out_tokens = (residual + (share_o + share_x)).astype(BF)

    ff_o = over_cores(core, ff_o)
    ff_x = over_cores(core, ff_x)
    ff_sum = ff_o + lax.ppermute(ff_x.astype(BF), "tensor", SWAP).astype(F32)
    ff_all = over_chips(core, ff_sum)

    d_norm2 = d_norm2_o + d_norm2_x
    grad_norm2 = jnp.sum(d_norm2 * normed_two, axis=0)
    d_res = out_grad.astype(F32) + norm_back(d_norm2, norm2_gain, normed_two, factor_two)
    d_attn = d_res.astype(BF)

    def back(q, k, v, mixed, lse, wout, wqkv):
        dm = mm_nt(d_attn, wout).astype(BF)
        dq, dk, dv = attn_back(scal, q, k, v, dm, lse, cos, sin)
        grads = jnp.concatenate(
            [
                mm_tn(norm1[:rows], dq).astype(BF),
                mm_tn(norm1, dk).astype(BF),
                mm_tn(norm1, dv).astype(BF),
                mm_tn(d_attn, mixed).astype(BF),
            ],
            axis=1,
        )
        d_norm = mm_nt(dk, wqkv[1]) + mm_nt(dv, wqkv[2])
        d_norm_q = mm_nt(dq, wqkv[0])
        return grads, d_norm, d_norm_q

    at_x, dn_x, dnq_x = back(q_x, k_x, v_x, mixed_x, lse_x, w_out_x, w_qkv_x)
    at_x = over_cores(core, at_x)
    at_recv = lax.ppermute(at_x.astype(BF), "tensor", SWAP).astype(F32)
    at_o, dn_o, dnq_o = back(q_o, k_o, v_o, mixed_o, lse_o, w_out, w_qkv)

    d_norm1_kv = dn_x + dn_o
    d_norm1_own = d_norm1_kv[:rows] + (dnq_x + dnq_o)
    d_norm1_halo = d_norm1_kv[rows:]
    grad_norm1 = jnp.sum(d_norm1_own * normed_one[:rows], axis=0) + jnp.sum(
        d_norm1_halo * normed_one[rows:], axis=0
    )
    norms = jnp.stack([grad_norm1, grad_norm2], axis=1)
    norms = norms + lax.ppermute(norms, "tensor", SWAP)
    at_o = jnp.concatenate([over_cores(core, at_o) + at_recv, over_cores(core, norms)], axis=1)
    at_all = over_chips(core, at_o)

    back_edge = lax.ppermute(d_norm1_halo, "tensor", SWAP)
    zeros = jnp.zeros((rows - HALF, width), F32)
    d_norm1 = d_norm1_own + jnp.where(
        tensor == 0,
        jnp.concatenate([zeros, back_edge], axis=0),
        jnp.concatenate([back_edge, zeros], axis=0),
    )
    in_grad = (
        d_res + norm_back(d_norm1, norm1_gain, normed_one[:rows], factor_one[:rows])
    ).astype(BF)

    heads = w_qkv.shape[2]
    grad_in = jnp.stack([ff_all[:, :ff], ff_all[:, ff : 2 * ff]]).astype(F32)
    grad_down = ff_all[:, 2 * ff :].astype(F32).T
    grad_qkv = jnp.stack([at_all[:, j * heads : (j + 1) * heads] for j in range(3)]).astype(F32)
    grad_out = at_all[:, 3 * heads : 4 * heads].astype(F32).T
    grad_norm1 = at_all[:, 4 * heads].astype(F32)
    grad_norm2 = at_all[:, 4 * heads + 1].astype(F32)
    return (out_tokens, in_grad, grad_norm1, grad_norm2, grad_qkv, grad_out, grad_in, grad_down)


def solution(mesh):
    chips = mesh.shape["dp"] // 2
    grid = Mesh(mesh.devices.reshape(chips, 2, 2), ("chip", "core", "tensor"))
    rows = P(("chip", "core", "tensor"), None)
    weights = (P(None, None, "tensor"), P("tensor", None), P(None, None, "tensor"), P("tensor", None))
    return jax.shard_map(
        per_device,
        mesh=grid,
        in_specs=(rows, P(("chip", "core"), None), P(), P(), *weights, rows),
        out_specs=(rows, rows, P(), P(), *weights),
        check_vma=False,
    )
```

time: 776 us -> 400 us (0.52)
  waiting for transfers between devices: 405 us -> 179 us
  matrix products: 131 us -> 45.8 us
  local copies, waits for them, and re-layouts: 97.8 us -> 37.7 us
  Pallas kernels: 0 us -> 42.1 us
  blocking collectives: 39.2 us -> 0 us
  starting transfers between devices: 0.62 us -> 37.9 us
  loops' own time: 19.8 us -> 0 us
  between operations: 14.8 us -> 2.91 us
    psum x1 -> x0, waiting for transfers between devices: 190 us -> none  [per_device(): lax.psum((grad_qkv, grad_out, grad_in, grad_down), 'dp')]
    all_gather x4 -> x0, waiting for transfers between devices: 132 us -> none  [the longest x1 35.6 us: per_device(): norm2_all = lax.all_gather(norm2_low, 'tensor', axis=0, tiled=True)]
    ppermute x0 -> x20, waiting for transfers between devices: none -> 100 us  [the longest x4 41.4 us: fetch(): across = lax.ppermute(pick(core, array, dim), 'tensor', SWAP)]
    dot_general x33 -> x36, matrix products: 131 us -> 45.8 us  [the longest x14 20.2 us: mm_nt(): lax.dot_general(a, b, (((1,), (1,)), ((), ())), preferred_element_type=F32)]
    reduce_scatter x4 -> x0, waiting for transfers between devices: 81.2 us -> none  [the longest x1 34.8 us: per_device(): lax.psum_scatter(back_product(d_up, w_in).astype(jnp.bfloat16), 'tensor',...]
    all_to_all x0 -> x4, waiting for transfers between devices: none -> 78.7 us  [the longest x2 49.4 us: over_chips(): full = lax.all_to_all(spread, 'chip', 0, 0).reshape(rows, width)]
    pallas_call x0 -> x4, Pallas kernels: none -> 42.1 us  [the longest x2 21.4 us: qkv_attn(): pl.pallas_call(qkv_attn_kernel, out_shape=(jax.ShapeDtypeStruct((rows, wi...]
    psum x1 -> x0, blocking collectives: 39.2 us -> none  [per_device(): lax.psum((grad_norm1, grad_norm2), ('dp', 'tensor'))]
  transfers between devices with their start and end apart: 9 -> 24, of which waited for: 8 -> 7; matrix products, arithmetic and copies ran while one was open for 6% -> 20% of each run, Pallas kernels for 0% -> 5%
where the time goes in v1:
time: 400 us; the launch traced here: 395 us
  waiting for transfers between devices  179 us (45%)
  other arithmetic  49.5 us (12%)
  matrix products  45.8 us (11%)
  Pallas kernels  42.1 us (11%)
  starting transfers between devices  37.9 us (9%)
  local copies, waits for them, and re-layouts  37.7 us (9%)
    all_to_all x2, waiting for transfers between devices, over_chips(): full = lax.all_to_all(spread, 'chip', 0, 0).reshape(rows, width)  49.4 us
    ppermute x4, waiting for transfers between devices, fetch(): across = lax.ppermute(pick(core, array, dim), 'tensor', SWAP)  41.4 us
    ppermute x1, waiting for transfers between devices, per_device(): ff_sum = ff_o + lax.ppermute(ff_x.astype(BF), 'tensor', SWAP).astype(F32)  29.4 us
    all_to_all x2, waiting for transfers between devices, over_chips(): pieces = lax.all_to_all(pieces, 'chip', 0, 0)  29.3 us
    ppermute x1, waiting for transfers between devices, per_device(): norms = norms + lax.ppermute(norms, 'tensor', SWAP)  25.3 us
    pallas_call x2, Pallas kernels, qkv_attn(): pl.pallas_call(qkv_attn_kernel, out_shape=(jax.ShapeDtypeStruct((rows, wi...  21.4 us
    pallas_call x2, Pallas kernels, attn_back(): pl.pallas_call(attn_back_kernel, out_shape=(jax.ShapeDtypeStruct((rows, w...  20.7 us
    dot_general x14, matrix products, mm_nt(): lax.dot_general(a, b, (((1,), (1,)), ((), ())), preferred_element_type=F32)  20.2 us
  transfers between devices with their start and end apart: 24, of which 7 were waited for; matrix products, arithmetic and copies ran while one was open for 20% of the time, Pallas kernels for 5%

profile of v1, /device:TPU:1, one launch (start us, length us, event | category | flops | bytes accessed | tf_op | source)
XLA Modules:
  0.0 395.0 jit_solution(1422163563756798299)
XLA Ops:
  20.1 41.4 %collective-permute-done.1 = bf16[3,384,384]{2,1,0:T(8,128)(2,1)} collective-permute-done((bf16[3,384,384]{2,1,0:T(8,128)(2,1)}, bf16[3,384,384]{2,1,0:T(8,128)(2,1)}, u32[]{:S(2)}, u32[]{:S(2)}) %collective-permute-start.1) | collective-permute-done | bytes 884768 | tf_op jit(solution)/shard_map/ppermute | solution.py:283
  64.8 10.8 %qkv_attn.2 = (bf16[768,384]{1,0:T(8,128)(2,1)S(1)}, bf16[896,384]{1,0:T(8,128)(2,1)S(1)}, bf16[896,384]{1,0:T(8,128)(2,1)S(1)}, bf16[768,384]{1,0:T(8,128)(2,1)S(1)}, f32[6,3,1,256]{3,2,1,0:T(1,128)S(1)}) custom-call(s32[4]{0:T(128)S(1)} %pad_add_fusion.1.scal_ref, bf16[832,768]{1,0:T(8,128)(2,1)S(1)} %get-tuple-element.114.norm_ref, ...), custom_call_target="tpu_custom_call" | custom-call | flops 2680160256 | bytes 8000000 | tf_op jit(solution)/shard_map/qkv_attn/pallas_call | solution.py:156
  81.2 10.6 %qkv_attn.3 = (bf16[768,384]{1,0:T(8,128)(2,1)S(1)}, bf16[896,384]{1,0:T(8,128)(2,1)S(1)}, bf16[896,384]{1,0:T(8,128)(2,1)S(1)}, bf16[768,384]{1,0:T(8,128)(2,1)S(1)}, f32[6,3,1,256]{3,2,1,0:T(1,128)S(1)}) custom-call(s32[4]{0:T(128)S(1)} %pad_add_fusion.1.scal_ref, bf16[832,768]{1,0:T(8,128)(2,1)S(1)} %get-tuple-element.114.norm_ref, ...), custom_call_target="tpu_custom_call" | custom-call | flops 2680160256 | bytes 8000000 | tf_op jit(solution)/shard_map/qkv_attn/pallas_call | solution.py:156
  103.8 2.7 multiply_convert_fusion.2
  117.0 10.3 %attn_back.3 = (bf16[768,384]{1,0:T(8,128)(2,1)S(1)}, bf16[832,384]{1,0:T(8,128)(2,1)S(1)}, bf16[832,384]{1,0:T(8,128)(2,1)S(1)}) custom-call(s32[4]{0:T(128)S(1)} %pad_add_fusion.1.scal_ref, bf16[768,384]{1,0:T(8,128)(2,1)S(1)} %get-tuple-element.32.q_ref, bf16[896,384]{1,0:T(8,128)(2,1)S(1)} %get-tuple-element.33.k_ref, ...), custom_call_target="tpu_custom_call" | custom-call | flops 3019898880 | bytes 8000000 | tf_op jit(solution)/shard_map/attn_back/pallas_call | solution.py:230
  134.1 10.4 %attn_back.2 = (bf16[768,384]{1,0:T(8,128)(2,1)S(1)}, bf16[832,384]{1,0:T(8,128)(2,1)S(1)}, bf16[832,384]{1,0:T(8,128)(2,1)S(1)}) custom-call(s32[4]{0:T(128)S(1)} %pad_add_fusion.1.scal_ref, bf16[768,384]{1,0:T(8,128)(2,1)S(1)} %get-tuple-element.26.q_ref, bf16[896,384]{1,0:T(8,128)(2,1)S(1)} %get-tuple-element.27.k_ref, ...), custom_call_target="tpu_custom_call" | custom-call | flops 3019898880 | bytes 8000000 | tf_op jit(solution)/shard_map/attn_back/pallas_call | solution.py:230
  156.4 4.2 %collective-permute-done.9 = f32[64,768]{1,0:T(8,128)S(1)} collective-permute-done((f32[64,768]{1,0:T(8,128)S(1)}, f32[64,768]{1,0:T(8,128)S(1)}, u32[]{:S(2)}, u32[]{:S(2)}) %collective-permute-start.9) | collective-permute-done | bytes 196640 | tf_op jit(solution)/shard_map/ppermute | solution.py:409
  160.6 2.8 multiply_reduce_fusion.1
  166.6 25.3 %collective-permute-done.13 = f32[768,2]{0,1:T(2,128)S(1)} collective-permute-done((f32[768,2]{0,1:T(2,128)S(1)}, f32[768,2]{0,1:T(2,128)S(1)}, u32[]{:S(2)}, u32[]{:S(2)}) %collective-permute-start.13) | collective-permute-done | bytes 6176 | tf_op jit(solution)/shard_map/ppermute | solution.py:405
  197.0 3.4 add_convert_fusion.2
  205.3 5.5 %all-to-all-start = ((bf16[8,48,1538]{2,1,0:T(8,128)(2,1)}), bf16[8,48,1538]{2,1,0:T(8,128)(2,1)}, u32[]{:S(2)}, u32[]{:S(2)}) async-start(bf16[8,48,1538]{2,1,0:T(8,128)(2,1)} %pad_maximum_fusion.5), calls=%async_computation | async-start | bytes 2555904 | tf_op jit(solution)/shard_map/all_to_all | solution.py:297
  213.3 29.4 %collective-permute-done.18 = bf16[384,1728]{0,1:T(8,128)(2,1)S(1)} collective-permute-done((bf16[384,1728]{0,1:T(8,128)(2,1)S(1)}, bf16[384,1728]{0,1:T(8,128)(2,1)S(1)}, u32[]{:S(2)}, u32[]{:S(2)}) %collective-permute-start.18) | collective-permute-done | bytes 1327136 | tf_op jit(solution)/shard_map/ppermute | solution.py:369
  247.1 5.1 %all-to-all-start.2 = ((bf16[8,48,1728]{2,1,0:T(8,128)(2,1)}), bf16[8,48,1728]{2,1,0:T(8,128)(2,1)S(1)}, u32[]{:S(2)}, u32[]{:S(2)}) async-start(bf16[8,48,1728]{2,1,0:T(8,128)(2,1)} %bitcast.134), calls=%async_computation.2 | async-start | bytes 2752512 | tf_op jit(solution)/shard_map/all_to_all | solution.py:297
  253.7 29.3 %all-to-all-done.2 = bf16[8,48,1728]{2,1,0:T(8,128)(2,1)S(1)} async-done(((bf16[8,48,1728]{2,1,0:T(8,128)(2,1)}), bf16[8,48,1728]{2,1,0:T(8,128)(2,1)S(1)}, u32[]{:S(2)}, u32[]{:S(2)}) %all-to-all-start.2) | async-done | bytes 1327136 | tf_op jit(solution)/shard_map/all_to_all | solution.py:297
  284.1 6.0 %all-to-all-start.1 = ((bf16[8,48,1538]{2,1,0:T(8,128)(2,1)}), bf16[8,48,1538]{2,1,0:T(8,128)(2,1)S(1)}, u32[]{:S(2)}, u32[]{:S(2)}) async-start(bf16[8,48,1538]{2,1,0:T(8,128)(2,1)} %broadcast_in_dim.21), calls=%async_computation.1 | async-start | bytes 2555904 | tf_op jit(solution)/shard_map/all_to_all | solution.py:300
  291.0 28.9 %all-to-all-done.1 = bf16[8,48,1538]{2,1,0:T(8,128)(2,1)S(1)} async-done(((bf16[8,48,1538]{2,1,0:T(8,128)(2,1)}), bf16[8,48,1538]{2,1,0:T(8,128)(2,1)S(1)}, u32[]{:S(2)}, u32[]{:S(2)}) %all-to-all-start.1) | async-done | bytes 1181216 | tf_op jit(solution)/shard_map/all_to_all | solution.py:300
  322.2 4.6 %all-to-all-start.3 = ((bf16[8,48,1728]{2,1,0:T(8,128)(2,1)}), bf16[8,48,1728]{2,1,0:T(8,128)(2,1)}, u32[]{:S(2)}, u32[]{:S(2)}) async-start(bf16[8,48,1728]{2,1,0:T(8,128)(2,1)} %broadcast_in_dim.22), calls=%async_computation.3 | async-start | bytes 2752512 | tf_op jit(solution)/shard_map/all_to_all | solution.py:300
  329.4 2.6 copy.104
  333.4 4.6 %add_convert_fusion.5 = bf16[768,768]{1,0:T(8,128)(2,1)} fusion(f32[768,768]{1,0:T(8,128)S(1)} %copy-done.3, f32[768,768]{1,0:T(8,128)} %fusion.60, bf16[768,576]{0,1:T(8,128)(2,1)} %copy-done.23, bf16[288,768]{1,0:T(8,128)(2,1)} %copy-done.22, bf16[288,768]{1,0:T(8,128)(2,1)} %collective-permute-done.7, pred[]{:T(512)S(6)} %eq.5), kind=kOutput, calls=%fused_computation.28 | convolution fusion | flops 685228032 | bytes 7667713 | tf_op jit(solution)/shard_map/dot_general | solution.py:258
  338.0 20.5 %all-to-all-done.3 = bf16[8,48,1728]{2,1,0:T(8,128)(2,1)} async-done(((bf16[8,48,1728]{2,1,0:T(8,128)(2,1)}), bf16[8,48,1728]{2,1,0:T(8,128)(2,1)}, u32[]{:S(2)}, u32[]{:S(2)}) %all-to-all-start.3) | async-done | bytes 1327136 | tf_op jit(solution)/shard_map/all_to_all | solution.py:300
  363.2 3.8 add_convert_fusion.4
  374.9 3.1 maximum_convert_fusion.1
  385.8 3.7 maximum_convert_fusion
  389.5 5.3 %copy.112 = f32[2,768,576]{1,2,0:T(8,128)} copy(f32[2,768,576]{2,1,0:T(8,128)} %maximum_convert_fusion) | data formatting | bytes 7077888
  (195 shorter events, 117.6 us)
Async XLA Ops:
  2.4 15.1 %collective-permute-start = (bf16[64,768]{1,0:T(8,128)(2,1)}, bf16[64,768]{1,0:T(8,128)(2,1)}, u32[]{:S(2)}, u32[]{:S(2)}) collective-permute-start(bf16[64,768]{1,0:T(8,128)(2,1)} %slice_select_fusion), channel_id=1, source_target_pairs={{0,1},{1,0},{2,3},{3,2},{4,5},{5,4},{6,7},{7,6},{8,9},{9,8},{10,11... | collective-permute-start | bytes 294920 | tf_op jit(solution)/shard_map/ppermute | solution.py:314
  6.2 70.2 %collective-permute-start.3 = (bf16[192,768]{1,0:T(8,128)(2,1)}, bf16[192,768]{1,0:T(8,128)(2,1)}, u32[]{:S(2)}, u32[]{:S(2)}) collective-permute-start(bf16[192,768]{1,0:T(8,128)(2,1)} %constant_dynamic-slice_fusion.8), channel_id=1, source_target_pairs={{0,1},{1,0},{2,3},{3,2},{4,5},{5,4},{6,7},{7,6},{8,9},{9,8},{10,11... | collective-permute-start | bytes 884744 | tf_op jit(solution)/shard_map/ppermute | solution.py:283
  7.0 57.7 %collective-permute-start.7 = (bf16[288,768]{1,0:T(8,128)(2,1)}, bf16[288,768]{1,0:T(8,128)(2,1)}, u32[]{:S(2)}, u32[]{:S(2)}) collective-permute-start(bf16[288,768]{1,0:T(8,128)(2,1)} %constant_dynamic-slice_fusion.6), channel_id=1, source_target_pairs={{0,1},{1,0},{2,3},{3,2},{4,5},{5,4},{6,7},{7,6},{8,9},{9,8},{10,11... | collective-permute-start | bytes 1327112 | tf_op jit(solution)/shard_map/ppermute | solution.py:283
  9.7 67.2 %collective-permute-start.5 = (bf16[2,384,576]{1,2,0:T(8,128)(2,1)S(1)}, bf16[2,384,576]{1,2,0:T(8,128)(2,1)}, u32[]{:S(2)}, u32[]{:S(2)}) collective-permute-start(bf16[2,384,576]{1,2,0:T(8,128)(2,1)S(1)} %constant_dynamic-slice_fusion.7), channel_id=1, source_target_pairs={{0,1},{1,0},{2,3},{3,2},{4,5},{5,4},{6,7},{7,6},{8,9},{9,8},{10,11... | collective-permute-start | bytes 2654216 | tf_op jit(solution)/shard_map/ppermute | solution.py:283
  10.8 50.6 %collective-permute-start.1 = (bf16[3,384,384]{2,1,0:T(8,128)(2,1)}, bf16[3,384,384]{2,1,0:T(8,128)(2,1)}, u32[]{:S(2)}, u32[]{:S(2)}) collective-permute-start(bf16[3,384,384]{2,1,0:T(8,128)(2,1)} %constant_dynamic-slice_fusion.9), channel_id=1, source_target_pairs={{0,1},{1,0},{2,3},{3,2},{4,5},{5,4},{6,7},{7,6},{8,9},{9,8},{10,11... | collective-permute-start | bytes 2654216 | tf_op jit(solution)/shard_map/ppermute | solution.py:283
  61.4 17.8 %collective-permute-start.2 = (bf16[3,384,384]{2,1,0:T(8,128)(2,1)}, bf16[3,384,384]{2,1,0:T(8,128)(2,1)S(1)}, u32[]{:S(2)}, u32[]{:S(2)}) collective-permute-start(bf16[3,384,384]{2,1,0:T(8,128)(2,1)} %collective-permute-done.1), channel_id=1, source_target_pairs={{0,2},{2,0},{1,3},{3,1},{4,6},{6,4},{5,7},{7,5},{8,10},{10,8},{9,1... | collective-permute-start | bytes 2654216 | tf_op jit(solution)/shard_map/ppermute | solution.py:284
  64.7 12.3 %collective-permute-start.8 = (bf16[288,768]{1,0:T(8,128)(2,1)}, bf16[288,768]{1,0:T(8,128)(2,1)S(1)}, u32[]{:S(2)}, u32[]{:S(2)}) collective-permute-start(bf16[288,768]{1,0:T(8,128)(2,1)} %collective-permute-done.7), channel_id=1, source_target_pairs={{0,2},{2,0},{1,3},{3,1},{4,6},{6,4},{5,7},{7,5},{8,10},{10,8},{9,1... | collective-permute-start | bytes 1327112 | tf_op jit(solution)/shard_map/ppermute | solution.py:284
  76.4 15.5 %collective-permute-start.4 = (bf16[192,768]{1,0:T(8,128)(2,1)}, bf16[192,768]{1,0:T(8,128)(2,1)S(1)}, u32[]{:S(2)}, u32[]{:S(2)}) collective-permute-start(bf16[192,768]{1,0:T(8,128)(2,1)} %collective-permute-done.3), channel_id=1, source_target_pairs={{0,2},{2,0},{1,3},{3,1},{4,6},{6,4},{5,7},{7,5},{8,10},{10,8},{9,1... | collective-permute-start | bytes 884744 | tf_op jit(solution)/shard_map/ppermute | solution.py:284
  76.9 18.1 %collective-permute-start.6 = (bf16[2,384,576]{1,2,0:T(8,128)(2,1)}, bf16[2,384,576]{1,2,0:T(8,128)(2,1)S(1)}, u32[]{:S(2)}, u32[]{:S(2)}) collective-permute-start(bf16[2,384,576]{1,2,0:T(8,128)(2,1)} %collective-permute-done.5), channel_id=1, source_target_pairs={{0,2},{2,0},{1,3},{3,1},{4,6},{6,4},{5,7},{7,5},{8,10},{10,8},{9,1... | collective-permute-start | bytes 2654216 | tf_op jit(solution)/shard_map/ppermute | solution.py:284
  148.5 62.4 %collective-permute-start.17 = (bf16[384,1728]{0,1:T(8,128)(2,1)}, bf16[384,1728]{0,1:T(8,128)(2,1)}, u32[]{:S(2)}, u32[]{:S(2)}) collective-permute-start(bf16[384,1728]{0,1:T(8,128)(2,1)} %constant_dynamic-slice_fusion), channel_id=1, source_target_pairs={{0,2},{2,0},{1,3},{3,1},{4,6},{6,4},{5,7},{7,5},{8,10},{10,8},{9,1... | collective-permute-start | bytes 3981320 | tf_op jit(solution)/shard_map/ppermute | solution.py:289
  152.6 10.9 %collective-permute-start.11 = (bf16[384,1536]{0,1:T(8,128)(2,1)S(1)}, bf16[384,1536]{0,1:T(8,128)(2,1)S(1)}, u32[]{:S(2)}, u32[]{:S(2)}) collective-permute-start(bf16[384,1536]{0,1:T(8,128)(2,1)S(1)} %constant_dynamic-slice_fusion.4), channel_id=1, source_target_pairs={{0,2},{2,0},{1,3},{3,1},{4,6},{6,4},{5,7},{7,5},{8,10},{10,8},{9,1... | collective-permute-start | bytes 3538952 | tf_op jit(solution)/shard_map/ppermute | solution.py:289
  152.7 44.2 %collective-permute-start.10 = (bf16[384,1536]{0,1:T(8,128)(2,1)}, bf16[384,1536]{0,1:T(8,128)(2,1)}, u32[]{:S(2)}, u32[]{:S(2)}) collective-permute-start(bf16[384,1536]{0,1:T(8,128)(2,1)} %constant_dynamic-slice_fusion.5), channel_id=1, source_target_pairs={{0,2},{2,0},{1,3},{3,1},{4,6},{6,4},{5,7},{7,5},{8,10},{10,8},{9,1... | collective-permute-start | bytes 3538952 | tf_op jit(solution)/shard_map/ppermute | solution.py:289
  154.1 6.5 %collective-permute-start.9 = (f32[64,768]{1,0:T(8,128)S(1)}, f32[64,768]{1,0:T(8,128)S(1)}, u32[]{:S(2)}, u32[]{:S(2)}) collective-permute-start(f32[64,768]{1,0:T(8,128)S(1)} %get-tuple-element.112), channel_id=1, source_target_pairs={{0,1},{1,0},{2,3},{3,2},{4,5},{5,4},{6,7},{7,6},{8,9},{9,8},{10,11... | collective-permute-start | bytes 589832 | tf_op jit(solution)/shard_map/ppermute | solution.py:409
  164.8 32.1 %collective-permute-start.12 = (bf16[384,1536]{0,1:T(8,128)(2,1)}, bf16[384,1536]{0,1:T(8,128)(2,1)}, u32[]{:S(2)}, u32[]{:S(2)}) collective-permute-start(bf16[384,1536]{0,1:T(8,128)(2,1)} %add_convert_fusion.3), channel_id=1, source_target_pairs={{0,1},{1,0},{2,3},{3,2},{4,5},{5,4},{6,7},{7,6},{8,9},{9,8},{10,11... | collective-permute-start | bytes 3538952 | tf_op jit(solution)/shard_map/ppermute | solution.py:395
  165.3 26.6 %collective-permute-start.13 = (f32[768,2]{0,1:T(2,128)S(1)}, f32[768,2]{0,1:T(2,128)S(1)}, u32[]{:S(2)}, u32[]{:S(2)}) collective-permute-start(f32[768,2]{0,1:T(2,128)S(1)} %pad_maximum_fusion.8), channel_id=1, source_target_pairs={{0,1},{1,0},{2,3},{3,2},{4,5},{5,4},{6,7},{7,6},{8,9},{9,8},{10,11... | collective-permute-start | bytes 18440 | tf_op jit(solution)/shard_map/ppermute | solution.py:405
  191.9 3.0 collective-permute-start.14
  194.9 18.4 %collective-permute-start.16 = (bf16[384,1728]{0,1:T(8,128)(2,1)}, bf16[384,1728]{0,1:T(8,128)(2,1)}, u32[]{:S(2)}, u32[]{:S(2)}) collective-permute-start(bf16[384,1728]{0,1:T(8,128)(2,1)} %constant_dynamic-slice_fusion.1), channel_id=1, source_target_pairs={{0,2},{2,0},{1,3},{3,1},{4,6},{6,4},{5,7},{7,5},{8,10},{10,8},{9,1... | collective-permute-start | bytes 3981320 | tf_op jit(solution)/shard_map/ppermute | solution.py:289
  205.3 41.7 %all-to-all-start = ((bf16[8,48,1538]{2,1,0:T(8,128)(2,1)}), bf16[8,48,1538]{2,1,0:T(8,128)(2,1)}, u32[]{:S(2)}, u32[]{:S(2)}) async-start(bf16[8,48,1538]{2,1,0:T(8,128)(2,1)} %pad_maximum_fusion.5), calls=%async_computation | async-start | bytes 2555904 | tf_op jit(solution)/shard_map/all_to_all | solution.py:297
  212.7 30.0 %collective-permute-start.18 = (bf16[384,1728]{0,1:T(8,128)(2,1)S(1)}, bf16[384,1728]{0,1:T(8,128)(2,1)S(1)}, u32[]{:S(2)}, u32[]{:S(2)}) collective-permute-start(bf16[384,1728]{0,1:T(8,128)(2,1)S(1)} %add_convert_fusion.1), channel_id=1, source_target_pairs={{0,1},{1,0},{2,3},{3,2},{4,5},{5,4},{6,7},{7,6},{8,9},{9,8},{10,11... | collective-permute-start | bytes 3981320 | tf_op jit(solution)/shard_map/ppermute | solution.py:369
  247.1 35.9 %all-to-all-start.2 = ((bf16[8,48,1728]{2,1,0:T(8,128)(2,1)}), bf16[8,48,1728]{2,1,0:T(8,128)(2,1)S(1)}, u32[]{:S(2)}, u32[]{:S(2)}) async-start(bf16[8,48,1728]{2,1,0:T(8,128)(2,1)} %bitcast.134), calls=%async_computation.2 | async-start | bytes 2752512 | tf_op jit(solution)/shard_map/all_to_all | solution.py:297
  284.1 35.8 %all-to-all-start.1 = ((bf16[8,48,1538]{2,1,0:T(8,128)(2,1)}), bf16[8,48,1538]{2,1,0:T(8,128)(2,1)S(1)}, u32[]{:S(2)}, u32[]{:S(2)}) async-start(bf16[8,48,1538]{2,1,0:T(8,128)(2,1)} %broadcast_in_dim.21), calls=%async_computation.1 | async-start | bytes 2555904 | tf_op jit(solution)/shard_map/all_to_all | solution.py:300
  322.2 36.3 %all-to-all-start.3 = ((bf16[8,48,1728]{2,1,0:T(8,128)(2,1)}), bf16[8,48,1728]{2,1,0:T(8,128)(2,1)}, u32[]{:S(2)}, u32[]{:S(2)}) async-start(bf16[8,48,1728]{2,1,0:T(8,128)(2,1)} %broadcast_in_dim.22), calls=%async_computation.3 | async-start | bytes 2752512 | tf_op jit(solution)/shard_map/all_to_all | solution.py:300
  332.0 35.0 %collective-permute-start.15 = (bf16[384,1538]{0,1:T(8,128)(2,1)}, bf16[384,1538]{0,1:T(8,128)(2,1)}, u32[]{:S(2)}, u32[]{:S(2)}) collective-permute-start(bf16[384,1538]{0,1:T(8,128)(2,1)} %copy.104), channel_id=1, source_target_pairs={{0,2},{2,0},{1,3},{3,1},{4,6},{6,4},{5,7},{7,5},{8,10},{10,8},{9,1... | collective-permute-start | bytes 3543560 | tf_op jit(solution)/shard_map/ppermute | solution.py:301
  361.0 17.0 %collective-permute-start.19 = (bf16[384,1728]{0,1:T(8,128)(2,1)}, bf16[384,1728]{0,1:T(8,128)(2,1)}, u32[]{:S(2)}, u32[]{:S(2)}) collective-permute-start(bf16[384,1728]{0,1:T(8,128)(2,1)} %copy.108), channel_id=1, source_target_pairs={{0,2},{2,0},{1,3},{3,1},{4,6},{6,4},{5,7},{7,5},{8,10},{10,8},{9,1... | collective-permute-start | bytes 3981320 | tf_op jit(solution)/shard_map/ppermute | solution.py:301
  (28 other events, 393.9 us)

commit v2 on v1

v2 whole, which is shorter than its diff:
```python
import functools

import jax
import jax.numpy as jnp
from jax import lax
from jax.experimental import pallas as pl
from jax.experimental.pallas import tpu as pltpu
from jax.sharding import Mesh, PartitionSpec as P

HEAD_DIM = 64
HALF = 64
QB = 128
WIN = QB + 2 * HALF
SWAP = [(0, 1), (1, 0)]
BF = jnp.bfloat16
F32 = jnp.float32


def vmem(megabytes):
    return pltpu.CompilerParams(vmem_limit_bytes=megabytes * 1024 * 1024)


def normalize(values):
    centred = values - jnp.mean(values, axis=-1, keepdims=True)
    factor = lax.rsqrt(jnp.mean(centred * centred, axis=-1, keepdims=True) + 1e-05)
    return (centred * factor, factor)


def norm_back(d_norm, gain_vec, normed, factor):
    scaled = d_norm * gain_vec
    return factor * (
        scaled
        - jnp.mean(scaled, axis=-1, keepdims=True)
        - normed * jnp.mean(scaled * normed, axis=-1, keepdims=True)
    )


def partner_lanes(values):
    lane = lax.broadcasted_iota(jnp.int32, values.shape, 1)
    lower = (lane & 32) == 0
    width = values.shape[1]
    return jnp.where(
        lower, pltpu.roll(values, width - 32, 1), pltpu.roll(values, 32, 1)
    )


def window_bias(scal_ref, block, rows):
    e0, e1, t0, h0 = scal_ref[1], scal_ref[2], scal_ref[3], scal_ref[4]
    j = block * QB + lax.broadcasted_iota(jnp.int32, (WIN, QB), 0)
    t = t0 + block * QB + lax.broadcasted_iota(jnp.int32, (WIN, QB), 1)
    u = jnp.where(
        j < HALF, h0 + j, jnp.where(j >= rows + HALF, h0 + j - rows - HALF, t0 + j - HALF)
    )
    seg_t = (t >= e0).astype(jnp.int32) + (t >= e1).astype(jnp.int32)
    seg_u = (u >= e0).astype(jnp.int32) + (u >= e1).astype(jnp.int32)
    allowed = (seg_t == seg_u) & (jnp.abs(t - u) <= HALF)
    bias = jnp.where(allowed, 0.0, -1e30).astype(F32)
    return jnp.concatenate([bias, bias], axis=1)


def stack_heads(pair):
    lower = lax.broadcasted_iota(jnp.int32, pair.shape, 1) < HEAD_DIM
    zero = jnp.zeros_like(pair)
    return jnp.concatenate(
        [jnp.where(lower, pair, zero), jnp.where(lower, zero, pair)], axis=0
    )


def unstack_columns(both):
    return jnp.concatenate(
        [both[:HEAD_DIM, :QB], both[HEAD_DIM:, QB:]], axis=0
    ).T


def dot(a, b, contract):
    return lax.dot_general(a, b, ((contract[0], contract[1]), ((), ())), preferred_element_type=F32)


class Stage:
    def __init__(self, core, sources, buffers, in_sems, results, out_bufs, out_sems):
        self.buffers, self.results, self.out_bufs, self.out_sems = (
            buffers, results, out_bufs, out_sems,
        )
        self.pending, self.sent = [], []
        sem = 0
        for refs, buffer in zip(sources, buffers):
            copies = []
            if len(refs) == 1:
                pairs = [(refs[0], buffer)]
            else:
                dim = refs[2]
                size = refs[0].shape[dim]
                pairs = []
                for ref, index in ((refs[0], core), (refs[1], 1 - core)):
                    at = [slice(None)] * len(buffer.shape)
                    at[dim] = pl.ds(pl.multiple_of(index * size, size), size)
                    pairs.append((ref, buffer.at[tuple(at)]))
            for source, target in pairs:
                copy = pltpu.make_async_copy(source, target, in_sems.at[sem])
                copy.start()
                copies.append(copy)
                sem += 1
            self.pending.append(copies)

    def take(self, *which):
        for k in which:
            for copy in self.pending[k]:
                copy.wait()
            self.pending[k] = []
        found = tuple(self.buffers[k] for k in which)
        return found if len(found) > 1 else found[0]

    def send(self, *which):
        for k in which:
            copy = pltpu.make_async_copy(self.out_bufs[k], self.results[k], self.out_sems.at[k])
            copy.start()
            self.sent.append(copy)

    def finish(self):
        for copy in self.sent:
            copy.wait()


def call(body, scalars, inputs, outs, scratch, name):
    inputs = [one if isinstance(one, tuple) else (one,) for one in inputs]
    flat, shapes = [], []
    for one in inputs:
        flat += list(one[:2])
        shape = list(one[0].shape)
        if len(one) == 3:
            shape[one[2]] *= 2
        shapes.append(pltpu.VMEM(tuple(shape), one[0].dtype))
    count, n_out, n_scal = len(flat), len(outs), len(scalars)

    def kernel(*refs):
        scal, refs = refs[:n_scal], refs[n_scal:]
        hbm, refs = refs[:count], refs[count:]
        results, refs = refs[:n_out], refs[n_out:]
        bufs, refs = refs[: len(inputs)], refs[len(inputs) :]
        out_bufs, refs = refs[:n_out], refs[n_out:]
        in_sems, out_sems, refs = refs[0], refs[1], refs[2:]
        sources, at = [], 0
        for one in inputs:
            if len(one) == 3:
                sources.append((hbm[at], hbm[at + 1], one[2]))
                at += 2
            else:
                sources.append((hbm[at],))
                at += 1
        stage = Stage(scal[0][0], sources, bufs, in_sems, results, out_bufs, out_sems)
        body(stage, scal, out_bufs, refs)
        stage.finish()

    return pl.pallas_call(
        kernel,
        out_shape=tuple(jax.ShapeDtypeStruct(shape, kind) for shape, kind in outs),
        in_specs=[pl.BlockSpec(memory_space=pltpu.SMEM)] * n_scal
        + [pl.BlockSpec(memory_space=pl.ANY)] * count,
        out_specs=(pl.BlockSpec(memory_space=pl.ANY),) * n_out,
        scratch_shapes=shapes
        + [pltpu.VMEM(shape, kind) for shape, kind in outs]
        + [pltpu.SemaphoreType.DMA((count,)), pltpu.SemaphoreType.DMA((n_out,))]
        + [pltpu.VMEM(shape, kind) for shape, kind in scratch],
        compiler_params=vmem(60),
        cost_estimate=pl.CostEstimate(flops=1000, bytes_accessed=1000, transcendentals=0),
        name=name,
    )(*scalars, *flat)


def qkv_attn(scal, w, norm=None, tables=None, tokens=None, halo=None, gain=None):
    first = tokens is not None
    width, dim = (w[0] if isinstance(w, tuple) else w).shape[2], w[0].shape[-2]
    if isinstance(w, tuple):
        dim *= 2
    rows = tokens.shape[0] if first else norm.shape[0] - HALF
    ext = rows + HALF
    pairs = width // 128
    step = 208 if ext % 208 == 0 else 64
    frequency = 10000.0 ** (-jnp.arange(0, HEAD_DIM, 2, dtype=F32) / HEAD_DIM)

    def body(stage, scalars, outs, scratch):
        (scal_ref,) = scalars
        q_ref, k_ref, v_ref, mixed_ref, mixedt_ref, lse_ref = outs[:6]
        (q_scr,) = scratch
        if first:
            norm_ref, cos_ref, sin_ref = outs[6:]
            freq_ref, tok_ref, halo_ref, gain_ref = stage.take(0, 1, 2, 3)

            def norm_rows(src_ref, src, dst):
                normed, _ = normalize(src_ref[src, :].astype(F32))
                norm_ref[dst, :] = (normed * gain_ref[...]).astype(BF)

            def norm_step(i, carry):
                at = pl.ds(pl.multiple_of(i * QB, QB), QB)
                norm_rows(tok_ref, at, at)
                return carry

            lax.fori_loop(0, rows // QB, norm_step, 0)
            norm_rows(halo_ref, slice(0, HALF), slice(rows, ext))
            stage.send(6)

            def angles(i, carry):
                at = pl.ds(pl.multiple_of(i * HALF, HALF), HALF)
                j = i * HALF + lax.broadcasted_iota(jnp.int32, (HALF, 128), 0)
                e0, e1 = scal_ref[1], scal_ref[2]
                t = jnp.where(j < rows, scal_ref[3] + j, scal_ref[4] + j - rows)
                opening = jnp.where(t >= e1, e1, jnp.where(t >= e0, e0, 0))
                angle = (t - opening).astype(F32) * freq_ref[...]
                lane = lax.broadcasted_iota(jnp.int32, (HALF, 128), 1)
                sine = jnp.sin(angle)
                cos_ref[at, :] = jnp.cos(angle)
                sin_ref[at, :] = jnp.where((lane & 32) == 0, -sine, sine)
                return carry

            lax.fori_loop(0, ext // HALF, angles, 0)
            stage.send(7, 8)
            w_ref = stage.take(4)
        else:
            norm_ref, cos_ref, sin_ref, w_ref = stage.take(0, 1, 2, 3)

        def project(i, carry):
            at = pl.ds(pl.multiple_of(i * step, 16), step)
            low = norm_ref[at, :]
            cosine, sine = cos_ref[at, :], sin_ref[at, :]
            raw_q = jnp.dot(low, w_ref[0], preferred_element_type=F32)
            raw_k = jnp.dot(low, w_ref[1], preferred_element_type=F32)
            raw_v = jnp.dot(low, w_ref[2], preferred_element_type=F32)
            out = pl.ds(pl.multiple_of(HALF + i * step, 16), step)
            for p in range(pairs):
                cols = slice(p * 128, (p + 1) * 128)
                part = raw_q[:, cols]
                turned = (part * cosine + partner_lanes(part) * sine).astype(BF)
                q_scr[at, cols] = turned * BF(HEAD_DIM**-0.5)
                part = raw_k[:, cols]
                k_ref[out, cols] = (part * cosine + partner_lanes(part) * sine).astype(BF)
            v_ref[out, :] = raw_v.astype(BF)
            return carry

        lax.fori_loop(0, ext // step, project, 0)
        q_ref[...] = q_scr[:rows, :]
        k_ref[:HALF, :] = k_ref[rows + HALF :, :]
        v_ref[:HALF, :] = v_ref[rows + HALF :, :]
        stage.send(0, 1, 2)

        def block(i, carry):
            bias = window_bias(scal_ref, i, rows)
            at = pl.ds(pl.multiple_of(i * QB, QB), QB)
            keys = pl.ds(pl.multiple_of(i * QB, QB), WIN)
            cols = [slice(p * 128, (p + 1) * 128) for p in range(pairs)]
            scores = [
                dot(k_ref[keys, c], stack_heads(q_ref[at, c]), ((1,), (1,))) + bias for c in cols
            ]
            peaks = [jnp.max(one, axis=0, keepdims=True) for one in scores]
            raws = [jnp.exp(one - peak) for one, peak in zip(scores, peaks)]
            totals = [jnp.sum(one, axis=0, keepdims=True) for one in raws]
            probs = [(one * (1.0 / total)).astype(BF) for one, total in zip(raws, totals)]
            both = [dot(v_ref[keys, c], one, ((0,), (0,))) for c, one in zip(cols, probs)]
            for p, c in enumerate(cols):
                flipped = jnp.concatenate(
                    [both[p][:HEAD_DIM, :QB], both[p][HEAD_DIM:, QB:]], axis=0
                )
                mixedt_ref[c, at] = flipped.astype(BF)
                mixed_ref[at, c] = flipped.T.astype(BF)
                lse_ref[i, p] = peaks[p] + jnp.log(totals[p])
            return carry

        lax.fori_loop(0, rows // QB, block, 0)
        stage.send(3, 4, 5)

    outs = [
        ((rows, width), BF),
        ((rows + 2 * HALF, width), BF),
        ((rows + 2 * HALF, width), BF),
        ((rows, width), BF),
        ((width, rows), BF),
        ((rows // QB, pairs, 1, 2 * QB), F32),
    ]
    if first:
        outs += [((ext, dim), BF), ((ext, 128), F32), ((ext, 128), F32)]
        inputs = [jnp.tile(frequency, 4).reshape(1, 128), tokens, halo, gain.reshape(1, dim), w]
    else:
        inputs = [norm, *tables, w]
    return call(body, [scal], inputs, outs, [((ext, width), BF)], "qkv_attn")


def store_rows(pieces, place, start, value):
    size, stop = pieces.shape[1], start + value.shape[0]
    row = start
    while row < stop:
        block, inside = divmod(row, size)
        count = min(size - inside, stop - row)
        part = value[row - start : row - start + count].astype(BF)
        pieces[block ^ place, inside : inside + count, :] = part
        row += count


def ffn(where, dy, win, wdown, gain, start=None, carry_in=None):
    last = start is None
    rows, dim = dy.shape
    ff = win[0].shape[1] * 2 if isinstance(win, tuple) else win.shape[1]
    height = -(-3 * ff // 256) * 64
    step = 256 if rows % 256 == 0 else 64

    def body(stage, scalars, outs, scratch):
        (where_ref,) = scalars
        act_s, d_s, pieces = scratch[:3]
        if last:
            n_ref, res_ref, gain_ref, win_ref, dy_ref, wd_ref, share_in, dn_in = stage.take(*range(8))
            a_ref, b_ref, out_ref, dres_ref, dattn_ref, gn_ref = outs
            gn_ref[...] = jnp.zeros_like(gn_ref)
        else:
            tok_ref, mo_ref, mx_ref, wo_ref, wx_ref, gain_ref, win_ref, dy_ref, wd_ref = stage.take(
                *range(9)
            )
            a_ref, b_ref, n_ref, res_ref, share_ref, dn_ref = outs

        def one(i, carry):
            at = pl.ds(pl.multiple_of(i * step, step), step)
            if last:
                low = n_ref[at, :]
            else:
                residual = tok_ref[at, :].astype(F32) + (
                    jnp.dot(mo_ref[at, :], wo_ref[...], preferred_element_type=F32)
                    + jnp.dot(mx_ref[at, :], wx_ref[...], preferred_element_type=F32)
                )
                res_ref[at, :] = residual
                low = (normalize(residual)[0] * gain_ref[...]).astype(BF)
                n_ref[at, :] = low
            up_in = dot(low, win_ref[0], ((1,), (1,)))
            gate = dot(low, win_ref[1], ((1,), (1,)))
            gelu_out, gelu_slope = gelu_parts(up_in)
            act = (gelu_out * gate).astype(BF)
            act_s[at, :] = act
            share = jnp.dot(act, wd_ref[...], preferred_element_type=F32)
            d_act = dot(dy_ref[at, :], wd_ref[...], ((1,), (1,)))
            d_up = (d_act * gate * gelu_slope).astype(BF)
            d_gate = (d_act * gelu_out).astype(BF)
            d_s[at, :ff] = d_up
            d_s[at, ff:] = d_gate
            dn = jnp.dot(d_up, win_ref[0], preferred_element_type=F32) + jnp.dot(
                d_gate, win_ref[1], preferred_element_type=F32
            )
            if last:
                residual = res_ref[at, :]
                out_ref[at, :] = (residual + (share_in[at, :] + share)).astype(BF)
                dn = dn + dn_in[at, :]
                normed, factor = normalize(residual)
                gn_ref[...] += jnp.sum((dn * normed).reshape(step // 8, 8, dim), axis=0)
                d_res = dy_ref[at, :].astype(F32) + norm_back(dn, gain_ref[...], normed, factor)
                dres_ref[at, :] = d_res
                dattn_ref[at, :] = d_res.astype(BF)
            else:
                share_ref[at, :] = share
                dn_ref[at, :] = dn
            return carry

        lax.fori_loop(0, rows // step, one, 0)
        stage.send(2, 3, 4, 5)
        place = where_ref[1]
        for c in range(0, 2 * ff, 384):
            value = dot(d_s[:, c : c + 384], n_ref[...], ((0,), (0,)))
            store_rows(pieces, place, c, value)
        store_rows(pieces, place, 2 * ff, dot(act_s[...], dy_ref[...], ((0,), (0,))))
        if 4 * height > 3 * ff:
            store_rows(pieces, place, 3 * ff, jnp.zeros((4 * height - 3 * ff, dim), F32))
        a_ref[...] = pieces[:2]
        b_ref[...] = pieces[2:]
        stage.send(0, 1)

    block = ((2, height, dim), BF)
    gain = gain.reshape(1, dim)
    if last:
        norm, residual, share, dn = carry_in
        inputs = [norm, residual, gain, win, dy, wdown, share, dn]
        outs = [((rows, dim), BF), ((rows, dim), F32), ((rows, dim), BF), ((8, dim), F32)]
    else:
        inputs = [*start, gain, win, dy, wdown]
        outs = [((rows, dim), BF)] + [((rows, dim), F32)] * 3
    return call(
        body,
        [where],
        inputs,
        [block, block, *outs],
        [((rows, ff), BF), ((rows, 2 * ff), BF), ((4, height, dim), BF)],
        "ffn",
    )


def attn_back(scal, where, blocks, saved, d_attn, wout, wqkv, norm, tables, earlier=None):
    q, k, v, mixed_t, lse = saved
    rows, width = q.shape
    dim = d_attn.shape[1]
    ext = rows + HALF
    pairs = width // 128
    height = dim // blocks
    step = 256 if rows % 256 == 0 else 64

    def body(stage, scalars, outs, scratch):
        where_ref, scal_ref = scalars
        a_ref, b_ref, dn_ref = outs
        dk_acc, dv_acc, dm_s, dq_s, dk_s, dv_s, pieces = scratch
        dk_acc[...] = jnp.zeros_like(dk_acc)
        dv_acc[...] = jnp.zeros_like(dv_acc)
        da_ref, wo_ref = stage.take(0, 1)

        def mix_back(i, carry):
            at = pl.ds(pl.multiple_of(i * step, step), step)
            dm_s[at, :] = dot(da_ref[at, :], wo_ref[...], ((1,), (1,))).astype(BF)
            return carry

        lax.fori_loop(0, rows // step, mix_back, 0)
        q_ref, k_ref, v_ref, lse_ref, cos_ref, sin_ref = stage.take(*range(2, 8))

        def unrotate(part, at):
            return (part * cos_ref[at, :] - partner_lanes(part) * sin_ref[at, :]).astype(BF)

        def block(i, carry):
            bias = window_bias(scal_ref, i, rows)
            at = pl.ds(pl.multiple_of(i * QB, QB), QB)
            keys = pl.ds(pl.multiple_of(i * QB, QB), WIN)
            cols = [slice(p * 128, (p + 1) * 128) for p in range(pairs)]
            qs = [stack_heads(q_ref[at, c]) for c in cols]
            dms = [stack_heads(dm_s[at, c]) for c in cols]
            scores = [dot(k_ref[keys, c], one, ((1,), (1,))) + bias for c, one in zip(cols, qs)]
            d_probs = [dot(v_ref[keys, c], one, ((1,), (1,))) for c, one in zip(cols, dms)]
            probs = [jnp.exp(one - lse_ref[i, p]) for p, one in enumerate(scores)]
            dots = [jnp.sum(a * b, axis=0, keepdims=True) for a, b in zip(probs, d_probs)]
            d_scores = [(a * (b - c)).astype(BF) for a, b, c in zip(probs, d_probs, dots)]
            d_values = [dot(a.astype(BF), b, ((1,), (0,))) for a, b in zip(probs, dms)]
            d_keys = [dot(a, b, ((1,), (0,))) for a, b in zip(d_scores, qs)]
            both = [dot(k_ref[keys, c], one, ((0,), (0,))) for c, one in zip(cols, d_scores)]
            for p, c in enumerate(cols):
                dv_acc[keys, c] += d_values[p]
                dk_acc[keys, c] += d_keys[p]
                dq_s[at, c] = unrotate(unstack_columns(both[p]) * HEAD_DIM**-0.5, at)
            return carry

        lax.fori_loop(0, rows // QB, block, 0)
        dk_acc[rows + HALF :, :] += dk_acc[:HALF, :]
        dv_acc[rows + HALF :, :] += dv_acc[:HALF, :]

        def finish(i, carry):
            at = pl.ds(pl.multiple_of(i * HALF, HALF), HALF)
            src = pl.ds(pl.multiple_of(HALF + i * HALF, HALF), HALF)
            for p in range(pairs):
                c = slice(p * 128, (p + 1) * 128)
                dk_s[at, c] = unrotate(dk_acc[src, c], at)
            dv_s[at, :] = dv_acc[src, :].astype(BF)
            return carry

        lax.fori_loop(0, ext // HALF, finish, 0)
        norm_ref, mt_ref = stage.take(8, 9)
        low = norm_ref[...]
        me = where_ref[2]
        for j, value in enumerate((dq_s, dk_s, dv_s)):
            grad = dot(low[: value.shape[0]], value[...], ((0,), (0,))).astype(BF)
            for b in range(blocks):
                pieces[b ^ me, :, j * width : (j + 1) * width] = grad[b * height : (b + 1) * height]
        grad = jnp.dot(mt_ref[...], da_ref[...], preferred_element_type=F32).astype(BF)
        for b in range(blocks):
            half, row = divmod(b, blocks // 2)
            pieces[b ^ me, :, 3 * width :] = grad[
                row * height : (row + 1) * height, half * width : (half + 1) * width
            ]
        a_ref[...] = pieces[: blocks // 2]
        b_ref[...] = pieces[blocks // 2 :]
        stage.send(0, 1)
        w_ref = stage.take(10)
        if earlier is not None:
            dn_in = stage.take(11)

        def norm_grad(at, q_too):
            dn = dot(dk_s[at, :], w_ref[1], ((1,), (1,))) + dot(dv_s[at, :], w_ref[2], ((1,), (1,)))
            if q_too:
                dn = dn + dot(dq_s[at, :], w_ref[0], ((1,), (1,)))
            if earlier is not None:
                dn = dn + dn_in[at, :]
            dn_ref[at, :] = dn

        def norm_step(i, carry):
            norm_grad(pl.ds(pl.multiple_of(i * step, step), step), True)
            return carry

        lax.fori_loop(0, rows // step, norm_step, 0)
        norm_grad(slice(rows, ext), False)
        stage.send(2)

    block = ((blocks // 2, height, 4 * width), BF)
    inputs = [d_attn, wout, q, k, v, lse, *tables, norm, mixed_t, wqkv]
    if earlier is not None:
        inputs.append(earlier)
    return call(
        body,
        [where, scal],
        inputs,
        [block, block, ((ext, dim), F32)],
        [((rows + 2 * HALF, width), F32)] * 2
        + [((rows, width), BF)] * 2
        + [((ext, width), BF)] * 2
        + [((blocks, height, 4 * width), BF)],
        "attn_back",
    )


def gelu_parts(up_in):
    cdf_part = 0.5 * (1.0 + lax.erf(up_in * 0.7071067811865476))
    gelu_out = up_in * cdf_part
    gelu_slope = cdf_part + up_in * jnp.exp(-0.5 * up_in * up_in) * 0.3989422804014327
    return (gelu_out, gelu_slope)


def together(*values):
    return lax.optimization_barrier(values)


def after(value, *others):
    return lax.optimization_barrier((value, *others))[0]


def pick(index, array, dim=0):
    size = array.shape[dim] // 2
    return lax.dynamic_slice_in_dim(array, index * size, size, dim)


def trade(array, axis):
    return lax.ppermute(array, axis, SWAP)


def add(kept, recv):
    return (kept.astype(F32) + recv.astype(F32)).astype(BF)


def add3(one, two, three):
    return (one.astype(F32) + two.astype(F32) + three.astype(F32)).astype(BF)


def adds(kept, recv):
    half = kept.shape[0] // 2
    first, second = add(kept[:half], recv[:half]), add(kept[half:], recv[half:])
    return (first[0], second[0]) if half == 1 else (first, second)


def split(results):
    return results[2], results[:2]


def flip(array, bit):
    count = lax.axis_size("hi")
    return lax.ppermute(array, "hi", [(i, i ^ bit) for i in range(count)])


def deal(array):
    count = lax.axis_size("hi")
    rows, width = array.shape
    return lax.all_to_all(array.reshape(count, rows // count, width), "hi", 0, 0)


def total(pieces):
    return jnp.sum(pieces.astype(F32), axis=0).astype(BF)


def spread_hi(piece):
    count = lax.axis_size("hi")
    full = lax.all_to_all(jnp.broadcast_to(piece[None], (count,) + piece.shape), "hi", 0, 0)
    return full.reshape((count * piece.shape[0],) + piece.shape[1:])


def assemble_ff(where, pieces, ff):
    height, dim = pieces[0].shape

    def body(stage, scalars, outs, scratch):
        (where_ref,) = scalars
        gi_ref, gd_ref = outs
        (whole,) = scratch
        for k in range(4):
            whole[where_ref[1] ^ k] = stage.take(k)[...]
        for out, index in ((0, 0), (0, 1), (1, 2)):
            row, stop = index * ff, (index + 1) * ff
            while row < stop:
                block, inside = divmod(row, height)
                count = min(height - inside, stop - row)
                part = whole[block, inside : inside + count, :].astype(F32)
                at = slice(row - index * ff, row - index * ff + count)
                if out == 0:
                    gi_ref[index, at, :] = part
                else:
                    gd_ref[at, :] = part
                row += count
        stage.send(0, 1)

    return call(
        body,
        [where],
        list(pieces),
        [((2, ff, dim), F32), ((ff, dim), F32)],
        [((4, height, dim), BF)],
        "assemble_ff",
    )


def assemble_attn(where, pieces, heads):
    count, height, width = pieces[0].shape
    blocks = 4 * count

    def body(stage, scalars, outs, scratch):
        (where_ref,) = scalars
        gq_ref, go_ref = outs
        (whole,) = scratch
        for k in range(4):
            piece = stage.take(k)
            for b in range(count):
                whole[where_ref[2] ^ (k * count + b)] = piece[b]
        for b in range(blocks):
            at = slice(b * height, (b + 1) * height)
            for j in range(3):
                gq_ref[j, at, :] = whole[b, :, j * heads : (j + 1) * heads].astype(F32)
        stage.send(0)
        for b in range(blocks):
            half, row = divmod(b, blocks // 2)
            go_ref[row * height : (row + 1) * height, half * heads : (half + 1) * heads] = whole[
                b, :, 3 * heads :
            ].astype(F32)
        stage.send(1)

    return call(
        body,
        [where],
        list(pieces),
        [((3, blocks * height, heads), F32), ((heads, 2 * heads), F32)],
        [((blocks, height, width), BF)],
        "assemble_attn",
    )


def per_device(
    tokens_in, seq_lengths, norm1_gain, norm2_gain, w_qkv, w_out, w_in, w_down, out_grad
):
    rows, width = tokens_in.shape
    tensor = lax.axis_index("tensor")
    core = lax.axis_index("core")
    lo = lax.axis_index("lo")
    place = 2 * core + lo
    chips = lax.axis_size("hi")
    hi = lax.axis_index("hi")
    w_in = jnp.swapaxes(w_in, 1, 2)
    me, bit = place, 1
    while bit < chips:
        me, bit = 2 * me + (hi // bit) % 2, 2 * bit
    where = jnp.stack([core, place, me]).astype(jnp.int32)

    edge = jnp.where(tensor == 0, tokens_in[rows - HALF :], tokens_in[:HALF])
    halo = trade(edge, "tensor")
    halo, w_qkv, w_out = together(halo, w_qkv, w_out)
    qkv_across = trade(pick(core, w_qkv, 1), "tensor")
    out_across = trade(pick(core, w_out), "tensor")

    lengths = seq_lengths[0]
    own0 = tensor * rows
    halo0 = jnp.where(tensor == 0, rows, rows - HALF)
    scal = jnp.stack([core, lengths[0], lengths[0] + lengths[1], own0, halo0]).astype(jnp.int32)

    q_o, k_o, v_o, mixed_o, mixedt_o, lse_o, norm1, *tables = qkv_attn(
        scal, w_qkv, tokens=tokens_in, halo=halo, gain=norm1_gain
    )
    qkv_across, out_across, mixed_o = together(
        after(qkv_across, mixed_o), after(out_across, mixed_o), mixed_o
    )
    in_across = trade(after(pick(core, w_in, 1), mixed_o), "tensor")
    down_across = trade(after(pick(core, w_down), mixed_o), "tensor")
    w_qkv_x = (qkv_across, trade(qkv_across, "core"), 1)
    w_out_x = (out_across, trade(out_across, "core"), 0)
    q_x, k_x, v_x, mixed_x, mixedt_x, lse_x = qkv_attn(
        scal, (w_qkv_x[0], after(w_qkv_x[1], w_out_x[1]), 1), norm=norm1, tables=tables
    )

    ffa_o, ffb_o, norm2, residual, share, dn2 = ffn(
        where, out_grad, w_in, w_down, norm2_gain,
        start=(tokens_in, mixed_o, mixed_x, w_out, w_out_x),
    )
    share, dn2, ffa_o, ffb_o, in_across, down_across = together(
        share, dn2, ffa_o, ffb_o, after(in_across, ffa_o), after(down_across, ffa_o)
    )
    ff_o = adds(ffa_o, trade(ffb_o, "core"))
    w_in_x = (in_across, trade(in_across, "core"), 1)
    w_down_x = (down_across, trade(down_across, "core"), 0)
    ffo_side = trade(ff_o[1], "lo")
    w_in_x = (w_in_x[0], after(w_in_x[1], *ff_o), 1)
    ffa_x, ffb_x, out_tokens, d_res, d_attn, gain_two = ffn(
        where, out_grad, w_in_x, w_down_x, norm2_gain, carry_in=(norm2, residual, share, dn2)
    )
    out_tokens, d_res, d_attn, gain_two, ffa_x, ffb_x, ffo_side = together(
        out_tokens, d_res, d_attn, gain_two, ffa_x, ffb_x, after(ffo_side, ffa_x)
    )
    ff_o = add(ff_o[0], ffo_side)
    ff_x = adds(ffa_x, trade(ffb_x, "core"))
    ffx_side = trade(ff_x[1], "lo")
    d_attn = after(d_attn, *ff_x, ff_o)

    dn1, (ata_x, atb_x) = split(
        attn_back(
            scal, where, 4 * chips, (q_x, k_x, v_x, mixedt_x, lse_x), d_attn, w_out_x, w_qkv_x, norm1, tables
        )
    )
    dn1, ata_x, atb_x, ffx_side = together(dn1, ata_x, atb_x, after(ffx_side, ata_x))
    ff_x = add(ff_x[0], ffx_side)
    ff_recv = trade(ff_x, "tensor")
    at_x = adds(ata_x, trade(atb_x, "core"))
    atx_side = trade(at_x[1], "lo")
    q_o = after(q_o, *at_x, ff_x)
    dn1, (ata_o, atb_o) = split(
        attn_back(
            scal, where, 4 * chips, (q_o, k_o, v_o, mixedt_o, lse_o), d_attn, w_out, w_qkv, norm1, tables, dn1
        )
    )
    dn1, ata_o, atb_o, atx_side, ff_recv = together(
        dn1, ata_o, atb_o, after(atx_side, ata_o), after(ff_recv, ata_o)
    )
    at_o = adds(ata_o, trade(atb_o, "core"))
    ato_side = trade(at_o[1], "lo")
    at_x = add(at_x[0], atx_side)
    at_recv = trade(at_x, "tensor")
    ff_all = spread_hi(total(deal(add(ff_o, ff_recv))))

    at = add3(at_o[0], ato_side, at_recv)
    bit = 1
    while bit < chips:
        half = at.shape[0] // 2
        at = add(at[:half], flip(at[half:], bit))
        bit *= 2
    while bit > 1:
        bit //= 2
        at = jnp.concatenate([at, flip(at, bit)], axis=0)

    def gather(mine):
        side = trade(mine, "lo")
        return (mine, side, trade(mine, "core"), trade(side, "core"))

    grad_in, grad_down = assemble_ff(where, gather(ff_all), w_in.shape[1])
    grad_in = jnp.swapaxes(grad_in, 1, 2)
    grad_qkv, grad_out = assemble_attn(where, gather(at), w_qkv.shape[2])

    tokens_ext = jnp.concatenate([tokens_in, halo], axis=0).astype(F32)
    normed_one, factor_one = normalize(tokens_ext)
    norms = jnp.stack([jnp.sum(dn1 * normed_one, axis=0), jnp.sum(gain_two, axis=0)])
    everywhere = ("hi", "lo", "core", "tensor")
    spread = jnp.broadcast_to(norms[None], (lax.axis_size(everywhere), 2, width))
    norms = jnp.sum(lax.all_to_all(spread, everywhere, 0, 0), axis=0)

    back_edge = trade(dn1[rows:], "tensor")
    zeros = jnp.zeros((rows - HALF, width), F32)
    d_norm1 = dn1[:rows] + jnp.where(
        tensor == 0,
        jnp.concatenate([zeros, back_edge], axis=0),
        jnp.concatenate([back_edge, zeros], axis=0),
    )
    in_grad = (
        d_res + norm_back(d_norm1, norm1_gain, normed_one[:rows], factor_one[:rows])
    ).astype(BF)
    return (out_tokens, in_grad, norms[0], norms[1], grad_qkv, grad_out, grad_in, grad_down)


def solution(mesh):
    grid = Mesh(mesh.devices.reshape(mesh.shape["dp"] // 4, 2, 2, 2), ("hi", "lo", "core", "tensor"))
    rows = P(("hi", "lo", "core", "tensor"), None)
    weights = (P(None, None, "tensor"), P("tensor", None), P(None, None, "tensor"), P("tensor", None))
    return jax.shard_map(
        per_device,
        mesh=grid,
        in_specs=(rows, P(("hi", "lo", "core"), None), P(), P(), *weights, rows),
        out_specs=(rows, rows, P(), P(), *weights),
        check_vma=False,
    )
```

time: 400 us -> 263 us (0.66); the launches traced: 395 us -> 262 us
  waiting for transfers between devices: 179 us -> 71 us
  Pallas kernels: 42.1 us -> 106 us
  matrix products: 45.8 us -> 0 us
  local copies, waits for them, and re-layouts: 37.7 us -> 13.3 us
  other arithmetic: 49.5 us -> 26.2 us
  starting transfers between devices: 37.9 us -> 43.8 us
    all_to_all x4 -> x3, waiting for transfers between devices: 78.7 us -> 0.01 us  [the longest x1 0.01 us: deal(): lax.all_to_all(array.reshape(count, rows // count, width), 'hi', 0, 0)]
    pallas_call x4 -> x8, Pallas kernels: 42.1 us -> 106 us  [call(): pl.pallas_call(kernel, out_shape=tuple((jax.ShapeDtypeStruct(shape, kind)...]
    dot_general x36 -> x0, matrix products: 45.8 us -> none  [the longest x14 20.2 us: mm_nt(): lax.dot_general(a, b, (((1,), (1,)), ((), ())), preferred_element_type=F32)]
    ppermute x20 -> x30, waiting for transfers between devices: 100 us -> 71 us  [the longest x26 42.8 us: trade(): return lax.ppermute(array, axis, SWAP)]
    ppermute x20 -> x30, starting transfers between devices: 16.7 us -> 29.9 us  [the longest x26 23.7 us: trade(): return lax.ppermute(array, axis, SWAP)]
    unnamed x59 -> x56, local copies, waits for them, and re-layouts: 10 us -> 2.57 us
    all_to_all x4 -> x3, starting transfers between devices: 21.3 us -> 13.9 us  [the longest x1 6.33 us: per_device(): norms = jnp.sum(lax.all_to_all(spread, everywhere, 0, 0), axis=0)]
    select_n x4 -> x0, other arithmetic: 7.23 us -> none  [join(): jnp.where(core == 0, jnp.concatenate([mine, other], axis=dim), jnp.concat...]
  transfers between devices with their start and end apart: 24 -> 33, of which waited for: 7 -> 13; matrix products, arithmetic and copies ran while one was open for 20% -> 12% of each run, Pallas kernels for 5% -> 38%
where the time goes in v2:
time: 263 us; the launch traced here: 262 us
  Pallas kernels  106 us (40%)
  waiting for transfers between devices  71 us (27%)
  starting transfers between devices  43.8 us (17%)
  other arithmetic  26.2 us (10%)
  local copies, waits for them, and re-layouts  13.3 us (5%)
    pallas_call x8, Pallas kernels, call(): pl.pallas_call(kernel, out_shape=tuple((jax.ShapeDtypeStruct(shape, kind)...  106 us
    ppermute x26, waiting for transfers between devices, trade(): return lax.ppermute(array, axis, SWAP)  42.8 us
    ppermute x4, waiting for transfers between devices, flip(): return lax.ppermute(array, 'hi', [(i, i ^ bit) for i in range(count)])  28.2 us
    ppermute x26, starting transfers between devices, trade(): return lax.ppermute(array, axis, SWAP)  23.7 us
    convert_element_type x8, other arithmetic, add(): return (kept.astype(F32) + recv.astype(F32)).astype(BF)  7.71 us
    all_to_all x1, starting transfers between devices, per_device(): norms = jnp.sum(lax.all_to_all(spread, everywhere, 0, 0), axis=0)  6.33 us
    ppermute x4, starting transfers between devices, flip(): return lax.ppermute(array, 'hi', [(i, i ^ bit) for i in range(count)])  6.21 us
  transfers between devices with their start and end apart: 33, of which 13 were waited for; matrix products, arithmetic and copies ran while one was open for 12% of the time, Pallas kernels for 38%

profile of v2, /device:TPU:1, one launch (start us, length us, event | category | flops | bytes accessed | tf_op | source)
XLA Modules:
  0.0 262.5 jit_solution(614987091969794456)
XLA Ops:
  3.8 2.5 collective-permute-done.refs_3_
  14.4 13.6 %qkv_attn.2 = (bf16[768,384]{1,0:T(8,128)(2,1)}, bf16[896,384]{1,0:T(8,128)(2,1)}, bf16[896,384]{1,0:T(8,128)(2,1)}, bf16[768,384]{1,0:T(8,128)(2,1)}, bf16[384,...) custom-call(s32[5]{0:T(128)} %stack.41.refs_0_.refs_1_, ...), custom_call_target="tpu_custom_call" | custom-call | flops 1000 | bytes 1000 | tf_op jit(solution)/shard_map/qkv_attn/pallas_call | solution.py:154
  28.0 7.1 %collective-permute-done.2.refs_5_.refs_3_ = bf16[192,768]{1,0:T(8,128)(2,1)} collective-permute-done((bf16[192,768]{1,0:T(8,128)(2,1)S(1)}, bf16[192,768]{1,0:T(8,128)(2,1)}, u32[]{:S(2)}, u32[]{:S(2)}) %collective-permute-start.2) | collective-permute-done | bytes 294944 | tf_op jit(solution)/shard_map/ppermute | solution.py:526
  41.9 10.8 %qkv_attn.3 = (bf16[768,384]{1,0:T(8,128)(2,1)}, bf16[896,384]{1,0:T(8,128)(2,1)}, bf16[896,384]{1,0:T(8,128)(2,1)}, bf16[768,384]{1,0:T(8,128)(2,1)}, bf16[384,...) custom-call(s32[5]{0:T(128)} %stack.41.refs_0_.refs_1_, bf16[832,768]{1,0:T(8,128)(2,1)} %get-tuple-element.94.refs_1_.refs_11_.refs_10_, ...), custom_call_target="tpu_custom_call" | custom-call | flops 1000 | bytes 1000 | tf_op jit(solution)/shard_map/qkv_attn/pallas_call | solution.py:154
  52.7 17.5 %ffn.2 = (bf16[2,448,768]{2,1,0:T(8,128)(2,1)}, bf16[2,448,768]{2,1,0:T(8,128)(2,1)}, bf16[768,768]{1,0:T(8,128)(2,1)}, f32[768,768]{1,0:T(8,128)}, f32[768,768]{1,0:T(8,128)}, /*index=5*/f32[768,768]{1,0:T(8,128)}) custom-call(s32[3]{0:T(128)} %pad_add_fusion.refs_0_, bf16[768,768]{1,0:T(8,128)(2,1)} %refs_1_.1, ...), custom_call_target="tpu_custom_call" | custom-call | flops 1000 | bytes 1000 | tf_op jit(solution)/shard_map/ffn/pallas_call | solution.py:154
  70.8 3.9 %collective-permute-done.8 = bf16[2,448,768]{2,1,0:T(8,128)(2,1)S(1)} collective-permute-done((bf16[2,448,768]{2,1,0:T(8,128)(2,1)}, bf16[2,448,768]{2,1,0:T(8,128)(2,1)S(1)}, u32[]{:S(2)}, u32[]{:S(2)}) %collective-permute-start.8) | collective-permute-done | bytes 1376288 | tf_op jit(solution)/shard_map/ppermute | solution.py:526
  74.7 2.6 fusion.4
  80.5 17.4 %ffn.3 = (bf16[2,448,768]{2,1,0:T(8,128)(2,1)}, bf16[2,448,768]{2,1,0:T(8,128)(2,1)}, bf16[768,768]{1,0:T(8,128)(2,1)}, f32[768,768]{1,0:T(8,128)}, bf16[768,768]{1,0:T(8,128)(2,1)}, /*index=5*/f32[8,768]{1,0:T(8,128)}) custom-call(s32[3]{0:T(128)} %pad_add_fusion.refs_0_, bf16[768,768]{1,0:T(8,128)(2,1)} %get-tuple-element.101.refs_1_, ...), custom_call_target="tpu_custom_call" | custom-call | flops 1000 | bytes 1000 | tf_op jit(solution)/shard_map/ffn/pallas_call | solution.py:154
  98.4 3.0 %collective-permute-done.11 = bf16[2,448,768]{2,1,0:T(8,128)(2,1)S(1)} collective-permute-done((bf16[2,448,768]{2,1,0:T(8,128)(2,1)}, bf16[2,448,768]{2,1,0:T(8,128)(2,1)S(1)}, u32[]{:S(2)}, u32[]{:S(2)}) %collective-permute-start.11) | collective-permute-done | bytes 1376288 | tf_op jit(solution)/shard_map/ppermute | solution.py:526
  105.4 18.2 %attn_back.2 = (bf16[8,48,1536]{2,1,0:T(8,128)(2,1)}, bf16[8,48,1536]{2,1,0:T(8,128)(2,1)}, f32[832,768]{1,0:T(8,128)}) custom-call(s32[3]{0:T(128)} %pad_add_fusion.refs_0_, s32[5]{0:T(128)} %stack.41.refs_0_.refs_1_, bf16[768,768]{1,0:T(8,128)(2,1)} %get-tuple-element.131.refs_2_, bf16[192,768]{1,0:T(8,128)(2,1)} %collective-permute-done.2.refs_5_.refs_3_, ...), custom_call_target="tpu_custom_call" | custom-call | flops 1000 | bytes 1000 | tf_op jit(solution)/shard_map/attn_back/pallas_call | solution.py:154
  128.6 18.4 %attn_back.3 = (bf16[8,48,1536]{2,1,0:T(8,128)(2,1)}, bf16[8,48,1536]{2,1,0:T(8,128)(2,1)}, f32[832,768]{1,0:T(8,128)}) custom-call(s32[3]{0:T(128)} %pad_add_fusion.refs_0_, s32[5]{0:T(128)} %stack.41.refs_0_.refs_1_, bf16[768,768]{1,0:T(8,128)(2,1)} %get-tuple-element.131.refs_2_, bf16[384,768]{1,0:T(8,128)(2,1)} %refs_3_, ...), custom_call_target="tpu_custom_call" | custom-call | flops 1000 | bytes 1000 | tf_op jit(solution)/shard_map/attn_back/pallas_call | solution.py:154
  154.4 4.1 %all-to-all-start.1 = ((bf16[4,112,768]{2,1,0:T(8,128)(2,1)}), bf16[4,112,768]{2,1,0:T(8,128)(2,1)S(1)}, u32[]{:S(2)}, u32[]{:S(2)}) async-start(bf16[4,112,768]{2,1,0:T(8,128)(2,1)} %bitcast.13), calls=%async_computation.1 | async-start | bytes 1376256 | tf_op jit(solution)/shard_map/all_to_all | solution.py:555
  158.5 7.3 %collective-permute-done.19 = bf16[4,48,1536]{2,1,0:T(8,128)(2,1)} collective-permute-done((bf16[4,48,1536]{2,1,0:T(8,128)(2,1)}, bf16[4,48,1536]{2,1,0:T(8,128)(2,1)}, u32[]{:S(2)}, u32[]{:S(2)}) %collective-permute-start.19) | collective-permute-done | bytes 589856 | tf_op jit(solution)/shard_map/ppermute | solution.py:526
  171.2 8.5 %collective-permute-done.20 = bf16[2,48,1536]{2,1,0:T(8,128)(2,1)S(1)} collective-permute-done((bf16[2,48,1536]{2,1,0:T(8,128)(2,1)S(1)}, bf16[2,48,1536]{2,1,0:T(8,128)(2,1)S(1)}, u32[]{:S(2)}, u32[]{:S(2)}) %collective-permute-start.20) | collective-permute-done | bytes 294944 | tf_op jit(solution)/shard_map/ppermute | solution.py:549
  183.9 3.5 %all-to-all-start.2 = ((bf16[4,112,768]{2,1,0:T(8,128)(2,1)}), bf16[4,112,768]{2,1,0:T(8,128)(2,1)S(1)}, u32[]{:S(2)}, u32[]{:S(2)}) async-start(bf16[4,112,768]{2,1,0:T(8,128)(2,1)} %broadcast_in_dim.5), calls=%async_computation.2 | async-start | bytes 1376256 | tf_op jit(solution)/shard_map/all_to_all | solution.py:564
  191.5 19.7 %collective-permute-done.22 = bf16[1,48,1536]{2,1,0:T(8,128)(2,1)S(1)} collective-permute-done((bf16[1,48,1536]{2,1,0:T(8,128)(2,1)S(1)}, bf16[1,48,1536]{2,1,0:T(8,128)(2,1)S(1)}, u32[]{:S(2)}, u32[]{:S(2)}) %collective-permute-start.22) | collective-permute-done | bytes 147488 | tf_op jit(solution)/shard_map/ppermute | solution.py:549
  211.3 3.7 %multiply_reduce_fusion = (f32[768]{0:T(1024)S(1)}, f32[832,768]{1,0:T(8,128)}) fusion(f32[832,768]{1,0:T(8,128)} %get-tuple-element.156, f32[832]{0:T(1024)S(1)} %add_rsqrt_fusion, f32[832]{0:T(1024)S(1)} %broadcast_multiply_fusion.2, bf16[64,768]{1,0:T(8,128)(2,1)S(1)} %copy-done.10, bf16[768,768]{1,0:T(8,128)(2,1)S(1)} %copy-done), kind=kLoop, calls=%fused_computation.5 | loop fusion | flops 5111040 | bytes 6399488 | tf_op jit(solution)/shard_map/reduce_sum | solution.py:744
  215.9 6.3 %all-to-all-start = ((f32[32,2,768]{2,1,0:T(2,128)}), f32[32,2,768]{2,1,0:T(2,128)S(1)}, u32[]{:S(2)}, u32[]{:S(2)}) async-start(f32[32,2,768]{2,1,0:T(2,128)} %broadcast_in_dim.4), calls=%async_computation | async-start | bytes 393216 | tf_op jit(solution)/shard_map/all_to_all | solution.py:747
  225.0 5.3 %collective-permute-done.16 = f32[64,768]{1,0:T(8,128)S(1)} collective-permute-done((f32[64,768]{1,0:T(8,128)}, f32[64,768]{1,0:T(8,128)S(1)}, u32[]{:S(2)}, u32[]{:S(2)}) %collective-permute-start.16) | collective-permute-done | bytes 196640 | tf_op jit(solution)/shard_map/ppermute | solution.py:526
  230.3 3.0 %fusion.7 = (f32[768]{0:T(1024)S(1)}, f32[768]{0:T(1024)S(1)}) fusion(f32[768]{0:T(1024)S(1)} %copy-done.24, f32[64,768]{1,0:T(8,128)S(1)} %collective-permute-done.16, pred[]{:T(512)S(6)} %eq.8, f32[832,768]{1,0:T(8,128)} %get-tuple-element.156, f32[832,768]{1,0:T(8,128)} %get-tuple-element.177), kind=kLoop, calls=%fused_computation.30 | loop fusion | flops 3537408 | bytes 4924417 | tf_op jit(solution)/shard_map/reduce_sum | solution.py:33
  236.5 8.8 %collective-permute-done.24.refs_2_ = bf16[4,48,1536]{2,1,0:T(8,128)(2,1)} collective-permute-done((bf16[4,48,1536]{2,1,0:T(8,128)(2,1)S(1)}, bf16[4,48,1536]{2,1,0:T(8,128)(2,1)}, u32[]{:S(2)}, u32[]{:S(2)}) %collective-permute-start.24) | collective-permute-done | bytes 589856 | tf_op jit(solution)/shard_map/ppermute | solution.py:526
  247.7 3.1 %add_convert_fusion = bf16[768,768]{1,0:T(8,128)(2,1)} fusion(f32[768,768]{1,0:T(8,128)} %get-tuple-element.126, f32[832,768]{1,0:T(8,128)S(1)} %copy-done.2, f32[768]{0:T(1024)S(1)} %get-tuple-element.180, f32[768]{0:T(1024)S(1)} %get-tuple-element.181, f32[768]{0:T(1024)S(1)} %bitcast.26, f32[768]{0:T(1024)S(1)} %copy-done.24, ...), kind=kLoop, calls=%fused_computation.6 | loop fusion | flops 5308416 | bytes 8466433 | tf_op jit(solution)/shard_map/convert_element_type | solution.py:758
  252.4 5.1 %assemble_ff.1 = (f32[2,576,768]{2,1,0:T(8,128)}, f32[576,768]{1,0:T(8,128)}) custom-call(s32[3]{0:T(128)} %pad_add_fusion.refs_0_, bf16[448,768]{1,0:T(8,128)(2,1)} %bitcast.25, bf16[448,768]{1,0:T(8,128)(2,1)} %copy-done.17, bf16[448,768]{1,0:T(8,128)(2,1)} %copy-done.20, bf16[448,768]{1,0:T(8,128)(2,1)} %collective-permute-done.29.refs_4_), custom_call_target="tpu_custom_call" | custom-call | flops 1000 | bytes 1000 | tf_op jit(solution)/shard_map/assemble_ff/pallas_call | solution.py:154
  257.5 4.8 %assemble_attn.1 = (f32[3,768,384]{2,1,0:T(8,128)}, f32[384,768]{1,0:T(8,128)}) custom-call(s32[3]{0:T(128)} %pad_add_fusion.refs_0_, bf16[4,48,1536]{2,1,0:T(8,128)(2,1)} %copy-done.7, bf16[4,48,1536]{2,1,0:T(8,128)(2,1)} %collective-permute-done.24.refs_2_, bf16[4,48,1536]{2,1,0:T(8,128)(2,1)} %collective-permute-done.25.refs_3_, ...), custom_call_target="tpu_custom_call" | custom-call | flops 1000 | bytes 1000 | tf_op jit(solution)/shard_map/assemble_attn/pallas_call | solution.py:154
  (152 shorter events, 61.9 us)
Async XLA Ops:
  8.5 26.6 %collective-permute-start.1 = (bf16[3,384,384]{2,1,0:T(8,128)(2,1)}, bf16[3,384,384]{2,1,0:T(8,128)(2,1)S(1)}, u32[]{:S(2)}, u32[]{:S(2)}) collective-permute-start(bf16[3,384,384]{2,1,0:T(8,128)(2,1)} %constant_dynamic-slice_fusion.2), channel_id=1, source_target_pairs={{0,1},{1,0},{2,3},{3,2},{4,5},{5,4},{6,7},{7,6},{8,9},{9,8},{10,11... | collective-permute-start | bytes 2654216 | tf_op jit(solution)/shard_map/ppermute | solution.py:526
  9.5 25.6 %collective-permute-start.2 = (bf16[192,768]{1,0:T(8,128)(2,1)S(1)}, bf16[192,768]{1,0:T(8,128)(2,1)}, u32[]{:S(2)}, u32[]{:S(2)}) collective-permute-start(bf16[192,768]{1,0:T(8,128)(2,1)S(1)} %constant_dynamic-slice_fusion.1), channel_id=1, source_target_pairs={{0,1},{1,0},{2,3},{3,2},{4,5},{5,4},{6,7},{7,6},{8,9},{9,8},{10,11... | collective-permute-start | bytes 884744 | tf_op jit(solution)/shard_map/ppermute | solution.py:526
  38.2 31.9 %collective-permute-start.5 = (bf16[2,288,768]{2,1,0:T(8,128)(2,1)}, bf16[2,288,768]{2,1,0:T(8,128)(2,1)S(1)}, u32[]{:S(2)}, u32[]{:S(2)}) collective-permute-start(bf16[2,288,768]{2,1,0:T(8,128)(2,1)} %dynamic-slice_bitcast_fusion), channel_id=1, source_target_pairs={{0,1},{1,0},{2,3},{3,2},{4,5},{5,4},{6,7},{7,6},{8,9},{9,8},{10,11... | collective-permute-start | bytes 2654216 | tf_op jit(solution)/shard_map/ppermute | solution.py:526
  39.2 30.9 %collective-permute-start.6 = (bf16[288,768]{1,0:T(8,128)(2,1)S(1)}, bf16[288,768]{1,0:T(8,128)(2,1)S(1)}, u32[]{:S(2)}, u32[]{:S(2)}) collective-permute-start(bf16[288,768]{1,0:T(8,128)(2,1)S(1)} %constant_dynamic-slice_fusion), channel_id=1, source_target_pairs={{0,1},{1,0},{2,3},{3,2},{4,5},{5,4},{6,7},{7,6},{8,9},{9,8},{10,11... | collective-permute-start | bytes 1327112 | tf_op jit(solution)/shard_map/ppermute | solution.py:526
  70.7 7.6 %collective-permute-start.7 = (bf16[2,288,768]{2,1,0:T(8,128)(2,1)S(1)}, bf16[2,288,768]{2,1,0:T(8,128)(2,1)S(1)}, u32[]{:S(2)}, u32[]{:S(2)}) collective-permute-start(bf16[2,288,768]{2,1,0:T(8,128)(2,1)S(1)} %collective-permute-done.5.refs_4_), channel_id=1, source_target_pairs={{0,2},{2,0},{1,3},{3,1},{4,6},{6,4},{5,7},{7,5},{8,10},{10,8},{9,1... | collective-permute-start | bytes 2654216 | tf_op jit(solution)/shard_map/ppermute | solution.py:526
  77.2 20.7 %collective-permute-start.10 = (bf16[448,768]{1,0:T(8,128)(2,1)}, bf16[448,768]{1,0:T(8,128)(2,1)S(1)}, u32[]{:S(2)}, u32[]{:S(2)}) collective-permute-start(bf16[448,768]{1,0:T(8,128)(2,1)} %get-tuple-element.172), channel_id=1, source_target_pairs={{0,4},{4,0},{1,5},{5,1},{2,6},{6,2},{3,7},{7,3},{8,12},{12,8},{9,1... | collective-permute-start | bytes 2064392 | tf_op jit(solution)/shard_map/ppermute | solution.py:526
  103.1 20.6 %collective-permute-start.12 = (bf16[448,768]{1,0:T(8,128)(2,1)S(1)}, bf16[448,768]{1,0:T(8,128)(2,1)S(1)}, u32[]{:S(2)}, u32[]{:S(2)}) collective-permute-start(bf16[448,768]{1,0:T(8,128)(2,1)S(1)} %get-tuple-element.170), channel_id=1, source_target_pairs={{0,4},{4,0},{1,5},{5,1},{2,6},{6,2},{3,7},{7,3},{8,12},{12,8},{9,1... | collective-permute-start | bytes 2064392 | tf_op jit(solution)/shard_map/ppermute | solution.py:526
  125.4 21.6 %collective-permute-start.15 = (bf16[448,768]{1,0:T(8,128)(2,1)}, bf16[448,768]{1,0:T(8,128)(2,1)S(1)}, u32[]{:S(2)}, u32[]{:S(2)}) collective-permute-start(bf16[448,768]{1,0:T(8,128)(2,1)} %add_convert_fusion.2), channel_id=1, source_target_pairs={{0,1},{1,0},{2,3},{3,2},{4,5},{5,4},{6,7},{7,6},{8,9},{9,8},{10,11... | collective-permute-start | bytes 2064392 | tf_op jit(solution)/shard_map/ppermute | solution.py:526
  128.2 18.9 %collective-permute-start.14 = (bf16[4,48,1536]{2,1,0:T(8,128)(2,1)}, bf16[4,48,1536]{2,1,0:T(8,128)(2,1)}, u32[]{:S(2)}, u32[]{:S(2)}) collective-permute-start(bf16[4,48,1536]{2,1,0:T(8,128)(2,1)} %get-tuple-element.174), channel_id=1, source_target_pairs={{0,4},{4,0},{1,5},{5,1},{2,6},{6,2},{3,7},{7,3},{8,12},{12,8},{9,1... | collective-permute-start | bytes 1769480 | tf_op jit(solution)/shard_map/ppermute | solution.py:526
  150.6 15.2 %collective-permute-start.19 = (bf16[4,48,1536]{2,1,0:T(8,128)(2,1)}, bf16[4,48,1536]{2,1,0:T(8,128)(2,1)}, u32[]{:S(2)}, u32[]{:S(2)}) collective-permute-start(bf16[4,48,1536]{2,1,0:T(8,128)(2,1)} %add_convert_fusion.9), channel_id=1, source_target_pairs={{0,1},{1,0},{2,3},{3,2},{4,5},{5,4},{6,7},{7,6},{8,9},{9,8},{10,11... | collective-permute-start | bytes 1769480 | tf_op jit(solution)/shard_map/ppermute | solution.py:526
  153.1 14.9 %collective-permute-start.18 = (bf16[4,48,1536]{2,1,0:T(8,128)(2,1)}, bf16[4,48,1536]{2,1,0:T(8,128)(2,1)}, u32[]{:S(2)}, u32[]{:S(2)}) collective-permute-start(bf16[4,48,1536]{2,1,0:T(8,128)(2,1)} %add_convert_fusion.10), channel_id=1, source_target_pairs={{0,4},{4,0},{1,5},{5,1},{2,6},{6,2},{3,7},{7,3},{8,12},{12,8},{9,1... | collective-permute-start | bytes 1769480 | tf_op jit(solution)/shard_map/ppermute | solution.py:526
  154.4 28.5 %all-to-all-start.1 = ((bf16[4,112,768]{2,1,0:T(8,128)(2,1)}), bf16[4,112,768]{2,1,0:T(8,128)(2,1)S(1)}, u32[]{:S(2)}, u32[]{:S(2)}) async-start(bf16[4,112,768]{2,1,0:T(8,128)(2,1)} %bitcast.13), calls=%async_computation.1 | async-start | bytes 1376256 | tf_op jit(solution)/shard_map/all_to_all | solution.py:555
  169.7 10.0 %collective-permute-start.20 = (bf16[2,48,1536]{2,1,0:T(8,128)(2,1)S(1)}, bf16[2,48,1536]{2,1,0:T(8,128)(2,1)S(1)}, u32[]{:S(2)}, u32[]{:S(2)}) collective-permute-start(bf16[2,48,1536]{2,1,0:T(8,128)(2,1)S(1)} %slice.139), channel_id=1, source_target_pairs={{0,8},{8,0},{16,24},{24,16},{1,9},{9,1},{17,25},{25,17},{2,10},{10... | collective-permute-start | bytes 884744 | tf_op jit(solution)/shard_map/ppermute | solution.py:549
  183.9 31.1 %all-to-all-start.2 = ((bf16[4,112,768]{2,1,0:T(8,128)(2,1)}), bf16[4,112,768]{2,1,0:T(8,128)(2,1)S(1)}, u32[]{:S(2)}, u32[]{:S(2)}) async-start(bf16[4,112,768]{2,1,0:T(8,128)(2,1)} %broadcast_in_dim.5), calls=%async_computation.2 | async-start | bytes 1376256 | tf_op jit(solution)/shard_map/all_to_all | solution.py:564
  187.4 23.7 %collective-permute-start.22 = (bf16[1,48,1536]{2,1,0:T(8,128)(2,1)S(1)}, bf16[1,48,1536]{2,1,0:T(8,128)(2,1)S(1)}, u32[]{:S(2)}, u32[]{:S(2)}) collective-permute-start(bf16[1,48,1536]{2,1,0:T(8,128)(2,1)S(1)} %add_convert_fusion.15), channel_id=1, source_target_pairs={{0,16},{8,24},{16,0},{24,8},{1,17},{9,25},{17,1},{25,9},{2,18},{10... | collective-permute-start | bytes 442376 | tf_op jit(solution)/shard_map/ppermute | solution.py:549
  211.2 12.5 %collective-permute-start.23 = (bf16[2,48,1536]{2,1,0:T(8,128)(2,1)S(1)}, bf16[2,48,1536]{2,1,0:T(8,128)(2,1)S(1)}, u32[]{:S(2)}, u32[]{:S(2)}) collective-permute-start(bf16[2,48,1536]{2,1,0:T(8,128)(2,1)S(1)} %pad_maximum_fusion.2), channel_id=1, source_target_pairs={{0,8},{8,0},{16,24},{24,16},{1,9},{9,1},{17,25},{25,17},{2,10},{10... | collective-permute-start | bytes 884744 | tf_op jit(solution)/shard_map/ppermute | solution.py:549
  215.0 19.4 %collective-permute-start.27 = (bf16[448,768]{1,0:T(8,128)(2,1)S(1)}, bf16[448,768]{1,0:T(8,128)(2,1)S(1)}, u32[]{:S(2)}, u32[]{:S(2)}) collective-permute-start(bf16[448,768]{1,0:T(8,128)(2,1)S(1)} %bitcast.23), channel_id=1, source_target_pairs={{0,4},{4,0},{1,5},{5,1},{2,6},{6,2},{3,7},{7,3},{8,12},{12,8},{9,1... | collective-permute-start | bytes 2064392 | tf_op jit(solution)/shard_map/ppermute | solution.py:526
  215.9 35.0 %all-to-all-start = ((f32[32,2,768]{2,1,0:T(2,128)}), f32[32,2,768]{2,1,0:T(2,128)S(1)}, u32[]{:S(2)}, u32[]{:S(2)}) async-start(f32[32,2,768]{2,1,0:T(2,128)} %broadcast_in_dim.4), calls=%async_computation | async-start | bytes 393216 | tf_op jit(solution)/shard_map/all_to_all | solution.py:747
  222.2 8.1 %collective-permute-start.16 = (f32[64,768]{1,0:T(8,128)}, f32[64,768]{1,0:T(8,128)S(1)}, u32[]{:S(2)}, u32[]{:S(2)}) collective-permute-start(f32[64,768]{1,0:T(8,128)} %slice.115), channel_id=1, source_target_pairs={{0,1},{1,0},{2,3},{3,2},{4,5},{5,4},{6,7},{7,6},{8,9},{9,8},{10,11... | collective-permute-start | bytes 589832 | tf_op jit(solution)/shard_map/ppermute | solution.py:526
  223.7 21.6 %collective-permute-start.24 = (bf16[4,48,1536]{2,1,0:T(8,128)(2,1)S(1)}, bf16[4,48,1536]{2,1,0:T(8,128)(2,1)}, u32[]{:S(2)}, u32[]{:S(2)}) collective-permute-start(bf16[4,48,1536]{2,1,0:T(8,128)(2,1)S(1)} %pad_maximum_fusion.1.refs_1_), channel_id=1, source_target_pairs={{0,4},{4,0},{1,5},{5,1},{2,6},{6,2},{3,7},{7,3},{8,12},{12,8},{9,1... | collective-permute-start | bytes 1769480 | tf_op jit(solution)/shard_map/ppermute | solution.py:526
  233.3 18.3 %collective-permute-start.28 = (bf16[448,768]{1,0:T(8,128)(2,1)S(1)}, bf16[448,768]{1,0:T(8,128)(2,1)S(1)}, u32[]{:S(2)}, u32[]{:S(2)}) collective-permute-start(bf16[448,768]{1,0:T(8,128)(2,1)S(1)} %bitcast.24), channel_id=1, source_target_pairs={{0,2},{2,0},{1,3},{3,1},{4,6},{6,4},{5,7},{7,5},{8,10},{10,8},{9,1... | collective-permute-start | bytes 2064392 | tf_op jit(solution)/shard_map/ppermute | solution.py:526
  234.3 17.3 %collective-permute-start.29 = (bf16[448,768]{1,0:T(8,128)(2,1)S(1)}, bf16[448,768]{1,0:T(8,128)(2,1)}, u32[]{:S(2)}, u32[]{:S(2)}) collective-permute-start(bf16[448,768]{1,0:T(8,128)(2,1)S(1)} %collective-permute-done.27.refs_2_), channel_id=1, source_target_pairs={{0,2},{2,0},{1,3},{3,1},{4,6},{6,4},{5,7},{7,5},{8,10},{10,8},{9,1... | collective-permute-start | bytes 2064392 | tf_op jit(solution)/shard_map/ppermute | solution.py:526
  236.5 21.1 %collective-permute-start.25 = (bf16[4,48,1536]{2,1,0:T(8,128)(2,1)S(1)}, bf16[4,48,1536]{2,1,0:T(8,128)(2,1)}, u32[]{:S(2)}, u32[]{:S(2)}) collective-permute-start(bf16[4,48,1536]{2,1,0:T(8,128)(2,1)S(1)} %pad_maximum_fusion.1.refs_1_), channel_id=1, source_target_pairs={{0,2},{2,0},{1,3},{3,1},{4,6},{6,4},{5,7},{7,5},{8,10},{10,8},{9,1... | collective-permute-start | bytes 1769480 | tf_op jit(solution)/shard_map/ppermute | solution.py:526
  245.4 12.2 %collective-permute-start.26 = (bf16[4,48,1536]{2,1,0:T(8,128)(2,1)}, bf16[4,48,1536]{2,1,0:T(8,128)(2,1)}, u32[]{:S(2)}, u32[]{:S(2)}) collective-permute-start(bf16[4,48,1536]{2,1,0:T(8,128)(2,1)} %collective-permute-done.24.refs_2_), channel_id=1, source_target_pairs={{0,2},{2,0},{1,3},{3,1},{4,6},{6,4},{5,7},{7,5},{8,10},{10,8},{9,1... | collective-permute-start | bytes 1769480 | tf_op jit(solution)/shard_map/ppermute | solution.py:526
  (37 other events, 301.0 us)
